TPU v7x, 1024 devices: a whole 8x8x8 slice. The times are simulated.
1024 devices in a mesh: gx: 32 (over y_lo, z), gy: 16 (over x, y_hi), gz: 2 (over core).
Axes of the slice: x: 8, y: 8 (y_hi: 2, y_lo: 4; y = y_hi * 4 + y_lo), z: 8, core: 2. Of those that a mesh axis runs over, the one named last changes fastest.
Arguments:
- electric: float32 [3, 256, 256, 96], P(None, 'gx', 'gy', 'gz'), may hold values from -6 to 6
- magnetic: float32 [3, 256, 256, 96], P(None, 'gx', 'gy', 'gz'), may hold values from -6 to 6
- material: int32 [256, 256, 96], P('gx', 'gy', 'gz'), may hold values from 0 to 3
- permittivity: float32 [4], replicated, may hold values from 1 to 12
- source_cells: int32 [64, 3], replicated, may hold values from 0 to 255, as said below
- amplitudes: float32 [64, 3], replicated, may hold values from -16 to 16
- omegas: float32 [4], replicated, may hold values from 0.3 to 1.5
- design_mask: int32 [256, 8192], P('gx', ('gy', 'gz')), may hold values 0 or 1
- forward_dft: float32 [256, 24, 8192], P('gx', None, ('gy', 'gz')), may hold values from -6 to 6
- pixel_anchor: int32 [3], replicated, may hold values from 0 to 2
Outputs:
- adjoint_dft: float32 [256, 24, 8192], P('gx', None, ('gy', 'gz'))
- pixel_gradient: float32 [256, 8192], P('gx', ('gy', 'gz'))
- final_electric: float32 [3, 256, 256, 96], P(None, 'gx', 'gy', 'gz')
Inputs may be any that keep to these rules, and one draw needn't show every extreme that they name: `source_cells`: column 0 is below 256, column 1 below 256, column 2 below 96.
All inputs are finite; a program needn't handle non-finite values. No bound on the sum of `design_mask` on one device may be relied on, other than what follows from the above.
Results may differ from a plain program's by a relative error of at most 0.00011.
Values sent between devices are 32-bit elements; how exact they have to be, the bound alone decides.
A program may use at most 32 MiB of HBM per device.

v0:
```python
import math

import jax
import jax.numpy as jnp
from jax import lax
from jax.sharding import PartitionSpec as P

SLAB = 32
FREQ = 4
ITERS = 2
MATS = 4


COURANT = 0.5


def extended(cells, sides, width):
    for axis, dim in sides:
        count = lax.axis_size(axis)
        ends = count - 1
        head = lax.slice_in_dim(cells, 0, width, axis=dim)
        tail = lax.slice_in_dim(cells, cells.shape[dim] - width, cells.shape[dim], axis=dim)
        cells = jnp.concatenate(
            [
                lax.ppermute(tail, axis, [(i, (i + 1) % count) for i in range(ends)]),
                cells,
                lax.ppermute(head, axis, [((i + 1) % count, i) for i in range(ends)]),
            ],
            axis=dim,
        )
    return cells


def passed_along(array, axis, by):
    count = lax.axis_size(axis)
    pairs = [(i, i + by) for i in range(count) if 0 <= i + by < count]
    return lax.ppermute(array, axis, pairs)


def forward_diff(grid_field, direction):
    length = grid_field.shape[direction]
    following = jnp.concatenate(
        [
            lax.slice_in_dim(grid_field, 1, length, axis=direction),
            jnp.zeros_like(lax.slice_in_dim(grid_field, 0, 1, axis=direction)),
        ],
        axis=direction,
    )
    return following - grid_field


def backward_diff(grid_field, direction):
    length = grid_field.shape[direction]
    previous = jnp.concatenate(
        [
            jnp.zeros_like(lax.slice_in_dim(grid_field, 0, 1, axis=direction)),
            lax.slice_in_dim(grid_field, 0, length - 1, axis=direction),
        ],
        axis=direction,
    )
    return grid_field - previous


def magnetic_step(electric, magnetic):
    curl_x = forward_diff(electric[2], 1) - forward_diff(electric[1], 2)
    curl_y = forward_diff(electric[0], 2) - forward_diff(electric[2], 0)
    curl_z = forward_diff(electric[1], 0) - forward_diff(electric[0], 1)
    return magnetic - COURANT * jnp.stack([curl_x, curl_y, curl_z])


def electric_step(electric, magnetic, coefficient, source_term):
    curl_x = backward_diff(magnetic[2], 1) - backward_diff(magnetic[1], 2)
    curl_y = backward_diff(magnetic[0], 2) - backward_diff(magnetic[2], 0)
    curl_z = backward_diff(magnetic[1], 0) - backward_diff(magnetic[0], 1)
    return electric + coefficient * (jnp.stack([curl_x, curl_y, curl_z]) - source_term)


def spectral_weights(omegas, step_index):
    phases = omegas * (step_index + 1)
    return jnp.stack([jnp.cos(phases), -jnp.sin(phases)])


def accumulate(running, weights, slab_field):
    return running + weights[:, :, None, None, None, None] * slab_field[None, None]


def add_step(spectrum, slab_field, step_index, omegas):
    weights = spectral_weights(omegas, step_index)
    return accumulate(spectrum, weights, slab_field)


def arrange(spectrum):
    rows_x = spectrum.shape[3]
    return jnp.transpose(spectrum, (3, 0, 1, 2, 4, 5)).reshape(
        rows_x, 6 * FREQ, spectrum.shape[4] * spectrum.shape[5]
    )


def sensitivity(forward_dft, adjoint_dft, omegas, design_mask):
    product = (forward_dft * adjoint_dft).reshape(
        forward_dft.shape[0], 2, FREQ, 3, forward_dft.shape[2]
    )
    real_part = jnp.sum(product[:, 0] - product[:, 1], axis=2)
    return (
        0.05
        * jnp.sum((omegas * omegas)[None, :, None] * real_part, axis=1)
        * design_mask.astype(jnp.float32)
    )


def pixel_fold(padded, coords, offset, direction):
    length = padded.shape[direction] - 4
    view_shape = [1] * padded.ndim
    view_shape[direction] = length
    home_pixel = (coords + offset) // 3
    running = lax.slice_in_dim(padded, 2, 2 + length, axis=direction)
    for displacement in (-2, -1, 1, 2):
        neighbor = lax.slice_in_dim(
            padded, 2 + displacement, 2 + displacement + length, axis=direction
        )
        same_pixel = ((coords + displacement + offset) // 3 == home_pixel).reshape(view_shape)
        running = running + jnp.where(same_pixel, neighbor, 0.0)
    return running


def build_source(source_cells, amplitudes, coord_x, coord_y, coord_z):
    onehot_x = (coord_x[None, :] == source_cells[:, 0:1]).astype(jnp.float32)
    onehot_y = (coord_y[None, :] == source_cells[:, 1:2]).astype(jnp.float32)
    onehot_z = (coord_z[None, :] == source_cells[:, 2:3]).astype(jnp.float32)
    return jnp.einsum(
        "sc,sx,sy,sz->cxyz",
        amplitudes,
        onehot_x,
        onehot_y,
        onehot_z,
        precision=lax.Precision.HIGHEST,
    )


def body(
    electric,
    magnetic,
    material,
    permittivity,
    source_cells,
    amplitudes,
    omegas,
    design_mask,
    forward_dft,
    pixel_anchor,
):
    extent_x, extent_y, extent_z = (electric.shape[1], electric.shape[2], electric.shape[3])
    half_rows = extent_y // 2
    bottom = extent_z // 4
    start_x = lax.axis_index("gx") * extent_x
    start_y = lax.axis_index("gy") * extent_y
    start_z = lax.axis_index("gz") * extent_z
    total_x = extent_x * lax.axis_size("gx")
    total_y = extent_y * lax.axis_size("gy")
    total_z = extent_z * lax.axis_size("gz")
    lower_device = lax.axis_index("gz") == 0
    eps_cells = jnp.zeros(material.shape, jnp.float32)
    for level in range(MATS):
        eps_cells = eps_cells + jnp.where(material == level, permittivity[level], 0.0)
    coefficient = COURANT / eps_cells
    spectrum = jnp.zeros((2, FREQ, 3, extent_x, extent_y, SLAB), jnp.float32)
    depth = 1
    coefficient_pad = jnp.pad(coefficient, 1)
    coord_x = start_x - depth + jnp.arange(extent_x + 2 * depth, dtype=jnp.int32)
    coord_y = start_y - depth + jnp.arange(extent_y + 2 * depth, dtype=jnp.int32)
    coord_z = start_z - depth + jnp.arange(extent_z + 2 * depth, dtype=jnp.int32)
    inside_x = (coord_x >= 0) & (coord_x < total_x)
    inside_y = (coord_y >= 0) & (coord_y < total_y)
    inside_z = (coord_z >= 0) & (coord_z < total_z)
    inside = (inside_x[:, None, None] & inside_y[None, :, None] & inside_z[None, None, :]).astype(
        jnp.float32
    )
    source_field = build_source(source_cells, amplitudes, coord_x, coord_y, coord_z)
    fields = jnp.concatenate([electric, magnetic], axis=0)
    for block in range(ITERS // depth):
        padded = extended(fields, (("gx", 1), ("gy", 2), ("gz", 3)), depth)
        electric_pad = padded[:3]
        magnetic_pad = padded[3:]
        step_index = block * depth
        magnetic_pad = magnetic_step(electric_pad, magnetic_pad) * inside
        electric_pad = (
            electric_step(
                electric_pad,
                magnetic_pad,
                coefficient_pad,
                source_field * math.cos(0.7 * (step_index + 0.5)),
            )
            * inside
        )
        slab_field = electric_pad[
            :,
            depth : depth + extent_x,
            depth : depth + extent_y,
            depth + bottom : depth + bottom + SLAB,
        ]
        spectrum = add_step(spectrum, slab_field, step_index, omegas)
        fields = jnp.concatenate(
            [
                electric_pad[
                    :, depth : depth + extent_x, depth : depth + extent_y, depth : depth + extent_z
                ],
                magnetic_pad[
                    :, depth : depth + extent_x, depth : depth + extent_y, depth : depth + extent_z
                ],
            ],
            axis=0,
        )
    final_electric = fields[:3]
    lower_part = arrange(spectrum[:, :, :, :, :half_rows])
    upper_part = passed_along(arrange(spectrum[:, :, :, :, half_rows:]), "gz", 1)
    adjoint_dft = jnp.where(lower_device, lower_part, upper_part)
    gradient = sensitivity(forward_dft, adjoint_dft, omegas, design_mask).reshape(
        extent_x, half_rows, SLAB
    )
    padded_grad = extended(gradient, (("gx", 0), (("gy", "gz"), 1)), 2)
    coords_x = start_x + jnp.arange(extent_x, dtype=jnp.int32)
    folded = pixel_fold(padded_grad, coords_x, pixel_anchor[0], 0)
    coords_y = lax.axis_index(("gy", "gz")) * half_rows + jnp.arange(half_rows, dtype=jnp.int32)
    folded = pixel_fold(folded, coords_y, pixel_anchor[1], 1)
    folded = pixel_fold(
        jnp.pad(folded, ((0, 0), (0, 0), (2, 2))),
        jnp.arange(SLAB, dtype=jnp.int32),
        pixel_anchor[2],
        2,
    )
    return (adjoint_dft, folded.reshape(extent_x, half_rows * SLAB), final_electric)


def solution(mesh):
    return jax.shard_map(
        body,
        mesh=mesh,
        in_specs=(
            P(None, "gx", "gy", "gz"),
            P(None, "gx", "gy", "gz"),
            P("gx", "gy", "gz"),
            P(),
            P(),
            P(),
            P(),
            P("gx", ("gy", "gz")),
            P("gx", None, ("gy", "gz")),
            P(),
        ),
        out_specs=(P("gx", None, ("gy", "gz")), P("gx", ("gy", "gz")), P(None, "gx", "gy", "gz")),
        check_vma=False,
    )
```

profile of v0, /device:TPU:23, one launch (start us, length us, event | category | flops | bytes accessed | tf_op | source)
XLA Modules:
  0.0 120.9 jit_solution(12444056280878068188)
XLA Ops:
  0.7 1.1 pad_maximum_fusion.4
  1.8 4.9 %collective-permute-start = (f32[6,1,16,48]{3,2,0,1:T(8,128)S(1)}, f32[6,1,16,48]{3,2,0,1:T(8,128)S(1)}, u32[]{:S(2)}, u32[]{:S(2)}) collective-permute-start(f32[6,1,16,48]{3,2,0,1:T(8,128)S(1)} %copy.132), channel_id=1, source_target_pairs={{0,32},{32,64},{64,96},{96,128},{128,160},{160,192},{192,224},{224... | collective-permute-start | bytes 55304 | tf_op jit(solution)/shard_map/ppermute | solution.py:25
  6.7 13.8 %collective-permute-start.1 = (f32[6,1,16,48]{3,2,0,1:T(8,128)S(1)}, f32[6,1,16,48]{3,2,0,1:T(8,128)S(1)}, u32[]{:S(2)}, u32[]{:S(2)}) collective-permute-start(f32[6,1,16,48]{3,2,0,1:T(8,128)S(1)} %copy.133), channel_id=1, source_target_pairs={{32,0},{64,32},{96,64},{128,96},{160,128},{192,160},{224,192},{256... | collective-permute-start | bytes 55304 | tf_op jit(solution)/shard_map/ppermute | solution.py:27
  20.7 1.4 %fusion.43 = (f32[1]{0:T(128)}, f32[1]{0:T(128)}, f32[1]{0:T(128)}, f32[1]{0:T(128)}) fusion(f32[4]{0:T(128)} %param.13), kind=kLoop, calls=%fused_computation.159 | loop fusion | bytes 32 | tf_op jit(solution)/shard_map/slice | solution.py:164
  22.1 0.8 slice_bitcast_fusion.22
  23.2 3.4 %add_divide_fusion = f32[8,16,48]{2,1,0:T(8,128)S(1)} fusion(s32[8,16,48]{2,1,0:T(8,128)} %param.12, f32[]{:T(128)} %bitcast.5, f32[]{:T(128)} %bitcast.4, f32[]{:T(128)} %bitcast.3, f32[]{:T(128)} %bitcast.2), kind=kLoop, calls=%fused_computation.76 | loop fusion | flops 73728 | bytes 49168 | tf_op jit(solution)/shard_map/div | solution.py:165
  26.9 7.9 %collective-permute-start.2 = (f32[6,10,1,48]{3,2,0,1:T(1,128)S(1)}, f32[6,10,1,48]{3,2,0,1:T(1,128)S(1)}, u32[]{:S(2)}, u32[]{:S(2)}) collective-permute-start(f32[6,10,1,48]{3,2,0,1:T(1,128)S(1)} %get-tuple-element.38), channel_id=1, source_target_pairs={{0,2},{2,4},{4,6},{6,8},{8,10},{10,12},{12,14},{14,16},{16,18},{18... | collective-permute-start | bytes 34568 | tf_op jit(solution)/shard_map/ppermute | solution.py:25
  34.8 2.2 %collective-permute-start.3 = (f32[6,10,1,48]{3,2,0,1:T(1,128)S(1)}, f32[6,10,1,48]{3,2,0,1:T(1,128)S(1)}, u32[]{:S(2)}, u32[]{:S(2)}) collective-permute-start(f32[6,10,1,48]{3,2,0,1:T(1,128)S(1)} %get-tuple-element.39), channel_id=1, source_target_pairs={{2,0},{4,2},{6,4},{8,6},{10,8},{12,10},{14,12},{16,14},{18,16},{20... | collective-permute-start | bytes 34568 | tf_op jit(solution)/shard_map/ppermute | solution.py:27
  37.1 6.3 %collective-permute-done.3 = f32[6,10,1,48]{3,2,0,1:T(1,128)S(1)} collective-permute-done((f32[6,10,1,48]{3,2,0,1:T(1,128)S(1)}, f32[6,10,1,48]{3,2,0,1:T(1,128)S(1)}, u32[]{:S(2)}, u32[]{:S(2)}) %collective-permute-start.3) | collective-permute-done | bytes 11552 | tf_op jit(solution)/shard_map/ppermute | solution.py:27
  43.3 0.1 pad_maximum_fusion
  43.5 0.3 fusion.37
  43.8 0.5 copy.69
  44.2 1.3 %collective-permute-start.4 = (f32[6,10,18,1]{2,3,1,0:T(1,128)S(1)}, f32[6,10,18,1]{2,3,1,0:T(1,128)S(1)}, u32[]{:S(2)}, u32[]{:S(2)}) collective-permute-start(f32[6,10,18,1]{2,3,1,0:T(1,128)S(1)} %copy.69), channel_id=1, source_target_pairs={{0,1},{2,3},{4,5},{6,7},{8,9},{10,11},{12,13},{14,15},{16,17},{18,... | collective-permute-start | bytes 12968 | tf_op jit(solution)/shard_map/ppermute | solution.py:25
  45.5 0.5 copy.70
  46.0 4.3 %collective-permute-start.5 = (f32[6,10,18,1]{2,3,1,0:T(1,128)S(1)}, f32[6,10,18,1]{2,3,1,0:T(1,128)S(1)}, u32[]{:S(2)}, u32[]{:S(2)}) collective-permute-start(f32[6,10,18,1]{2,3,1,0:T(1,128)S(1)} %copy.70), channel_id=1, source_target_pairs={{1,0},{3,2},{5,4},{7,6},{9,8},{11,10},{13,12},{15,14},{17,16},{19,... | collective-permute-start | bytes 12968 | tf_op jit(solution)/shard_map/ppermute | solution.py:27
  50.3 0.6 fusion.42
  51.0 0.5 copy.71
  51.4 0.5 copy.72
  51.9 0.6 pad_maximum_fusion.1
  53.1 0.1 slice.451
  53.2 0.2 subtract_bitcast_fusion.8
  53.4 0.3 copy-done.5
  53.7 0.5 fusion.3
  54.2 0.1 slice.450
  54.3 1.9 %collective-permute-start.6 = (f32[6,1,16,48]{3,2,0,1:T(8,128)S(1)}, f32[6,1,16,48]{3,2,0,1:T(8,128)S(1)}, u32[]{:S(2)}, u32[]{:S(2)}) collective-permute-start(f32[6,1,16,48]{3,2,0,1:T(8,128)S(1)} %get-tuple-element.40), channel_id=1, source_target_pairs={{0,32},{32,64},{64,96},{96,128},{128,160},{160,192},{192,224},{224... | collective-permute-start | bytes 55304 | tf_op jit(solution)/shard_map/ppermute | solution.py:25
  56.3 5.5 %collective-permute-start.7 = (f32[6,1,16,48]{3,2,0,1:T(8,128)S(1)}, f32[6,1,16,48]{3,2,0,1:T(8,128)S(1)}, u32[]{:S(2)}, u32[]{:S(2)}) collective-permute-start(f32[6,1,16,48]{3,2,0,1:T(8,128)S(1)} %get-tuple-element.41), channel_id=1, source_target_pairs={{32,0},{64,32},{96,64},{128,96},{160,128},{192,160},{224,192},{256... | collective-permute-start | bytes 55304 | tf_op jit(solution)/shard_map/ppermute | solution.py:27
  61.8 1.1 collective-permute-done.7
  63.0 5.5 %collective-permute-start.8 = (f32[6,10,1,48]{3,2,0,1:T(1,128)S(1)}, f32[6,10,1,48]{3,2,0,1:T(1,128)S(1)}, u32[]{:S(2)}, u32[]{:S(2)}) collective-permute-start(f32[6,10,1,48]{3,2,0,1:T(1,128)S(1)} %get-tuple-element.36), channel_id=1, source_target_pairs={{0,2},{2,4},{4,6},{6,8},{8,10},{10,12},{12,14},{14,16},{16,18},{18... | collective-permute-start | bytes 34568 | tf_op jit(solution)/shard_map/ppermute | solution.py:25
  68.5 4.6 %collective-permute-start.9 = (f32[6,10,1,48]{3,2,0,1:T(1,128)S(1)}, f32[6,10,1,48]{3,2,0,1:T(1,128)S(1)}, u32[]{:S(2)}, u32[]{:S(2)}) collective-permute-start(f32[6,10,1,48]{3,2,0,1:T(1,128)S(1)} %get-tuple-element.37), channel_id=1, source_target_pairs={{2,0},{4,2},{6,4},{8,6},{10,8},{12,10},{14,12},{16,14},{18,16},{20... | collective-permute-start | bytes 34568 | tf_op jit(solution)/shard_map/ppermute | solution.py:27
  73.1 0.7 fusion.32
  73.8 3.3 %collective-permute-done.9 = f32[6,10,1,48]{3,2,0,1:T(1,128)S(1)} collective-permute-done((f32[6,10,1,48]{3,2,0,1:T(1,128)S(1)}, f32[6,10,1,48]{3,2,0,1:T(1,128)S(1)}, u32[]{:S(2)}, u32[]{:S(2)}) %collective-permute-start.9) | collective-permute-done | bytes 11552 | tf_op jit(solution)/shard_map/ppermute | solution.py:27
  77.0 0.1 pad_maximum_fusion.2
  77.2 0.3 fusion.36
  77.4 0.5 copy.86
  77.9 1.3 %collective-permute-start.10 = (f32[6,10,18,1]{2,3,1,0:T(1,128)S(1)}, f32[6,10,18,1]{2,3,1,0:T(1,128)S(1)}, u32[]{:S(2)}, u32[]{:S(2)}) collective-permute-start(f32[6,10,18,1]{2,3,1,0:T(1,128)S(1)} %copy.86), channel_id=1, source_target_pairs={{0,1},{2,3},{4,5},{6,7},{8,9},{10,11},{12,13},{14,15},{16,17},{18,... | collective-permute-start | bytes 12968 | tf_op jit(solution)/shard_map/ppermute | solution.py:25
  79.2 0.5 copy.87
  79.7 4.5 %collective-permute-start.11 = (f32[6,10,18,1]{2,3,1,0:T(1,128)S(1)}, f32[6,10,18,1]{2,3,1,0:T(1,128)S(1)}, u32[]{:S(2)}, u32[]{:S(2)}) collective-permute-start(f32[6,10,18,1]{2,3,1,0:T(1,128)S(1)} %copy.87), channel_id=1, source_target_pairs={{1,0},{3,2},{5,4},{7,6},{9,8},{11,10},{13,12},{15,14},{17,16},{19,... | collective-permute-start | bytes 12968 | tf_op jit(solution)/shard_map/ppermute | solution.py:27
  84.2 0.7 fusion.34
  84.9 0.5 copy.88
  85.4 0.5 copy.89
  85.9 0.6 pad_maximum_fusion.3
  87.0 0.2 subtract_bitcast_fusion.2
  87.1 0.1 fusion.1
  87.3 0.7 multiply_add_fusion
  87.9 0.2 slice_bitcast_fusion
  88.2 0.2 reshape.313
  88.4 1.3 %collective-permute-start.12 = (f32[8,24,256]{2,0,1:T(8,128)S(1)}, f32[8,24,256]{2,0,1:T(8,128)S(1)}, u32[]{:S(2)}, u32[]{:S(2)}) collective-permute-start(f32[8,24,256]{2,0,1:T(8,128)S(1)} %reshape.313), channel_id=1, source_target_pairs={{0,1},{2,3},{4,5},{6,7},{8,9},{10,11},{12,13},{14,15},{16,17},{18,... | collective-permute-start | bytes 589832 | tf_op jit(solution)/shard_map/ppermute | solution.py:37
  89.7 0.7 fusion.28
  90.4 0.7 fusion.30
  91.0 0.2 reshape.312
  91.3 0.4 collective-permute-done.12
  92.0 1.9 %collective-permute-start.13 = (f32[2,8,32]{2,1,0:T(8,128)S(1)}, f32[2,8,32]{2,1,0:T(8,128)S(1)}, u32[]{:S(2)}, u32[]{:S(2)}) collective-permute-start(f32[2,8,32]{2,1,0:T(8,128)S(1)} %slice.400), channel_id=1, source_target_pairs={{0,32},{32,64},{64,96},{96,128},{128,160},{160,192},{192,224},{224... | collective-permute-start | bytes 6152 | tf_op jit(solution)/shard_map/ppermute | solution.py:25
  93.9 0.7 fusion.24
  94.8 6.0 %collective-permute-start.14 = (f32[2,8,32]{2,1,0:T(8,128)S(1)}, f32[2,8,32]{2,1,0:T(8,128)S(1)}, u32[]{:S(2)}, u32[]{:S(2)}) collective-permute-start(f32[2,8,32]{2,1,0:T(8,128)S(1)} %slice.402), channel_id=1, source_target_pairs={{32,0},{64,32},{96,64},{128,96},{160,128},{192,160},{224,192},{256... | collective-permute-start | bytes 6152 | tf_op jit(solution)/shard_map/ppermute | solution.py:27
  100.8 0.7 collective-permute-done.14
  101.6 9.4 %collective-permute-start.15 = (f32[12,2,32]{2,1,0:T(2,128)S(1)}, f32[12,2,32]{2,1,0:T(2,128)S(1)}, u32[]{:S(2)}, u32[]{:S(2)}) collective-permute-start(f32[12,2,32]{2,1,0:T(2,128)S(1)} %get-tuple-element.60), channel_id=1, source_target_pairs={{0,1},{1,2},{2,3},{3,4},{4,5},{5,6},{6,7},{7,8},{8,9},{9,10},{10,1... | collective-permute-start | bytes 9224 | tf_op jit(solution)/shard_map/ppermute | solution.py:25
  110.9 1.9 %collective-permute-start.16 = (f32[12,2,32]{2,1,0:T(2,128)S(1)}, f32[12,2,32]{2,1,0:T(2,128)S(1)}, u32[]{:S(2)}, u32[]{:S(2)}) collective-permute-start(f32[12,2,32]{2,1,0:T(2,128)S(1)} %get-tuple-element.61), channel_id=1, source_target_pairs={{1,0},{2,1},{3,2},{4,3},{5,4},{6,5},{7,6},{8,7},{9,8},{10,9},{11,1... | collective-permute-start | bytes 9224 | tf_op jit(solution)/shard_map/ppermute | solution.py:27
  112.9 0.7 fusion.26
  113.5 0.1 slice.493
  113.6 0.7 copy.103
  114.3 0.7 copy.102
  115.1 4.8 %collective-permute-done.16 = f32[12,2,32]{2,1,0:T(2,128)S(1)} collective-permute-done((f32[12,2,32]{2,1,0:T(2,128)S(1)}, f32[12,2,32]{2,1,0:T(2,128)S(1)}, u32[]{:S(2)}, u32[]{:S(2)}) %collective-permute-start.16) | collective-permute-done | bytes 3104 | tf_op jit(solution)/shard_map/ppermute | solution.py:27
  119.9 0.1 fusion.12
  120.2 0.7 reshape.316
  (82 shorter events, 2.4 us)
Async XLA Ops:
  0.6 26.1 %copy-start.1 = (f32[3,8,16,48]{3,2,1,0:T(8,128)S(1)}, f32[3,8,16,48]{3,2,1,0:T(8,128)}, u32[]{:S(2)}) copy-start(f32[3,8,16,48]{3,2,1,0:T(8,128)} %param.10) | copy-start | bytes 221188
  0.6 26.1 %copy-start = (f32[3,8,16,48]{3,2,1,0:T(8,128)S(1)}, f32[3,8,16,48]{3,2,1,0:T(8,128)}, u32[]{:S(2)}) copy-start(f32[3,8,16,48]{3,2,1,0:T(8,128)} %param.11) | copy-start | bytes 221188
  0.7 36.3 %copy-start.6 = (f32[4]{0:T(128)S(1)}, f32[4]{0:T(128)}, u32[]{:S(2)}) copy-start(f32[4]{0:T(128)} %param.16) | copy-start | bytes 52
  1.8 24.9 %collective-permute-start = (f32[6,1,16,48]{3,2,0,1:T(8,128)S(1)}, f32[6,1,16,48]{3,2,0,1:T(8,128)S(1)}, u32[]{:S(2)}, u32[]{:S(2)}) collective-permute-start(f32[6,1,16,48]{3,2,0,1:T(8,128)S(1)} %copy.132), channel_id=1, source_target_pairs={{0,32},{32,64},{64,96},{96,128},{128,160},{160,192},{192,224},{224... | collective-permute-start | bytes 55304 | tf_op jit(solution)/shard_map/ppermute | solution.py:25
  6.7 20.1 %collective-permute-start.1 = (f32[6,1,16,48]{3,2,0,1:T(8,128)S(1)}, f32[6,1,16,48]{3,2,0,1:T(8,128)S(1)}, u32[]{:S(2)}, u32[]{:S(2)}) collective-permute-start(f32[6,1,16,48]{3,2,0,1:T(8,128)S(1)} %copy.133), channel_id=1, source_target_pairs={{32,0},{64,32},{96,64},{128,96},{160,128},{192,160},{224,192},{256... | collective-permute-start | bytes 55304 | tf_op jit(solution)/shard_map/ppermute | solution.py:27
  26.9 10.2 %collective-permute-start.2 = (f32[6,10,1,48]{3,2,0,1:T(1,128)S(1)}, f32[6,10,1,48]{3,2,0,1:T(1,128)S(1)}, u32[]{:S(2)}, u32[]{:S(2)}) collective-permute-start(f32[6,10,1,48]{3,2,0,1:T(1,128)S(1)} %get-tuple-element.38), channel_id=1, source_target_pairs={{0,2},{2,4},{4,6},{6,8},{8,10},{10,12},{12,14},{14,16},{16,18},{18... | collective-permute-start | bytes 34568 | tf_op jit(solution)/shard_map/ppermute | solution.py:25
  34.8 8.5 %collective-permute-start.3 = (f32[6,10,1,48]{3,2,0,1:T(1,128)S(1)}, f32[6,10,1,48]{3,2,0,1:T(1,128)S(1)}, u32[]{:S(2)}, u32[]{:S(2)}) collective-permute-start(f32[6,10,1,48]{3,2,0,1:T(1,128)S(1)} %get-tuple-element.39), channel_id=1, source_target_pairs={{2,0},{4,2},{6,4},{8,6},{10,8},{12,10},{14,12},{16,14},{18,16},{20... | collective-permute-start | bytes 34568 | tf_op jit(solution)/shard_map/ppermute | solution.py:27
  43.5 6.8 %copy-start.4 = (s32[3]{0:T(128)S(1)}, s32[3]{0:T(128)}, u32[]{:S(2)}) copy-start(s32[3]{0:T(128)} %param.19) | copy-start | bytes 40
  44.2 6.7 %collective-permute-start.4 = (f32[6,10,18,1]{2,3,1,0:T(1,128)S(1)}, f32[6,10,18,1]{2,3,1,0:T(1,128)S(1)}, u32[]{:S(2)}, u32[]{:S(2)}) collective-permute-start(f32[6,10,18,1]{2,3,1,0:T(1,128)S(1)} %copy.69), channel_id=1, source_target_pairs={{0,1},{2,3},{4,5},{6,7},{8,9},{10,11},{12,13},{14,15},{16,17},{18,... | collective-permute-start | bytes 12968 | tf_op jit(solution)/shard_map/ppermute | solution.py:25
  46.0 5.5 %collective-permute-start.5 = (f32[6,10,18,1]{2,3,1,0:T(1,128)S(1)}, f32[6,10,18,1]{2,3,1,0:T(1,128)S(1)}, u32[]{:S(2)}, u32[]{:S(2)}) collective-permute-start(f32[6,10,18,1]{2,3,1,0:T(1,128)S(1)} %copy.70), channel_id=1, source_target_pairs={{1,0},{3,2},{5,4},{7,6},{9,8},{11,10},{13,12},{15,14},{17,16},{19,... | collective-permute-start | bytes 12968 | tf_op jit(solution)/shard_map/ppermute | solution.py:27
  53.0 0.7 copy-start.5
  54.3 7.4 %collective-permute-start.6 = (f32[6,1,16,48]{3,2,0,1:T(8,128)S(1)}, f32[6,1,16,48]{3,2,0,1:T(8,128)S(1)}, u32[]{:S(2)}, u32[]{:S(2)}) collective-permute-start(f32[6,1,16,48]{3,2,0,1:T(8,128)S(1)} %get-tuple-element.40), channel_id=1, source_target_pairs={{0,32},{32,64},{64,96},{96,128},{128,160},{160,192},{192,224},{224... | collective-permute-start | bytes 55304 | tf_op jit(solution)/shard_map/ppermute | solution.py:25
  56.3 6.6 %collective-permute-start.7 = (f32[6,1,16,48]{3,2,0,1:T(8,128)S(1)}, f32[6,1,16,48]{3,2,0,1:T(8,128)S(1)}, u32[]{:S(2)}, u32[]{:S(2)}) collective-permute-start(f32[6,1,16,48]{3,2,0,1:T(8,128)S(1)} %get-tuple-element.41), channel_id=1, source_target_pairs={{32,0},{64,32},{96,64},{128,96},{160,128},{192,160},{224,192},{256... | collective-permute-start | bytes 55304 | tf_op jit(solution)/shard_map/ppermute | solution.py:27
  63.0 10.8 %collective-permute-start.8 = (f32[6,10,1,48]{3,2,0,1:T(1,128)S(1)}, f32[6,10,1,48]{3,2,0,1:T(1,128)S(1)}, u32[]{:S(2)}, u32[]{:S(2)}) collective-permute-start(f32[6,10,1,48]{3,2,0,1:T(1,128)S(1)} %get-tuple-element.36), channel_id=1, source_target_pairs={{0,2},{2,4},{4,6},{6,8},{8,10},{10,12},{12,14},{14,16},{16,18},{18... | collective-permute-start | bytes 34568 | tf_op jit(solution)/shard_map/ppermute | solution.py:25
  68.5 8.5 %collective-permute-start.9 = (f32[6,10,1,48]{3,2,0,1:T(1,128)S(1)}, f32[6,10,1,48]{3,2,0,1:T(1,128)S(1)}, u32[]{:S(2)}, u32[]{:S(2)}) collective-permute-start(f32[6,10,1,48]{3,2,0,1:T(1,128)S(1)} %get-tuple-element.37), channel_id=1, source_target_pairs={{2,0},{4,2},{6,4},{8,6},{10,8},{12,10},{14,12},{16,14},{18,16},{20... | collective-permute-start | bytes 34568 | tf_op jit(solution)/shard_map/ppermute | solution.py:27
  77.9 6.9 %collective-permute-start.10 = (f32[6,10,18,1]{2,3,1,0:T(1,128)S(1)}, f32[6,10,18,1]{2,3,1,0:T(1,128)S(1)}, u32[]{:S(2)}, u32[]{:S(2)}) collective-permute-start(f32[6,10,18,1]{2,3,1,0:T(1,128)S(1)} %copy.86), channel_id=1, source_target_pairs={{0,1},{2,3},{4,5},{6,7},{8,9},{10,11},{12,13},{14,15},{16,17},{18,... | collective-permute-start | bytes 12968 | tf_op jit(solution)/shard_map/ppermute | solution.py:25
  79.7 5.7 %collective-permute-start.11 = (f32[6,10,18,1]{2,3,1,0:T(1,128)S(1)}, f32[6,10,18,1]{2,3,1,0:T(1,128)S(1)}, u32[]{:S(2)}, u32[]{:S(2)}) collective-permute-start(f32[6,10,18,1]{2,3,1,0:T(1,128)S(1)} %copy.87), channel_id=1, source_target_pairs={{1,0},{3,2},{5,4},{7,6},{9,8},{11,10},{13,12},{15,14},{17,16},{19,... | collective-permute-start | bytes 12968 | tf_op jit(solution)/shard_map/ppermute | solution.py:27
  88.1 3.6 %copy-start.2 = (f32[8,24,256]{2,1,0:T(8,128)S(1)}, f32[8,24,256]{2,1,0:T(8,128)}, u32[]{:S(2)}) copy-start(f32[8,24,256]{2,1,0:T(8,128)} %param.18) | copy-start | bytes 589828
  88.1 3.8 %copy-start.3 = (s32[8,256]{1,0:T(8,128)S(1)}, s32[8,256]{1,0:T(8,128)}, u32[]{:S(2)}) copy-start(s32[8,256]{1,0:T(8,128)} %param.17) | copy-start | bytes 24580
  88.4 3.3 %collective-permute-start.12 = (f32[8,24,256]{2,0,1:T(8,128)S(1)}, f32[8,24,256]{2,0,1:T(8,128)S(1)}, u32[]{:S(2)}, u32[]{:S(2)}) collective-permute-start(f32[8,24,256]{2,0,1:T(8,128)S(1)} %reshape.313), channel_id=1, source_target_pairs={{0,1},{2,3},{4,5},{6,7},{8,9},{10,11},{12,13},{14,15},{16,17},{18,... | collective-permute-start | bytes 589832 | tf_op jit(solution)/shard_map/ppermute | solution.py:37
  92.0 8.8 %collective-permute-start.13 = (f32[2,8,32]{2,1,0:T(8,128)S(1)}, f32[2,8,32]{2,1,0:T(8,128)S(1)}, u32[]{:S(2)}, u32[]{:S(2)}) collective-permute-start(f32[2,8,32]{2,1,0:T(8,128)S(1)} %slice.400), channel_id=1, source_target_pairs={{0,32},{32,64},{64,96},{96,128},{128,160},{160,192},{192,224},{224... | collective-permute-start | bytes 6152 | tf_op jit(solution)/shard_map/ppermute | solution.py:25
  94.8 6.8 %collective-permute-start.14 = (f32[2,8,32]{2,1,0:T(8,128)S(1)}, f32[2,8,32]{2,1,0:T(8,128)S(1)}, u32[]{:S(2)}, u32[]{:S(2)}) collective-permute-start(f32[2,8,32]{2,1,0:T(8,128)S(1)} %slice.402), channel_id=1, source_target_pairs={{32,0},{64,32},{96,64},{128,96},{160,128},{192,160},{224,192},{256... | collective-permute-start | bytes 6152 | tf_op jit(solution)/shard_map/ppermute | solution.py:27
  101.6 13.5 %collective-permute-start.15 = (f32[12,2,32]{2,1,0:T(2,128)S(1)}, f32[12,2,32]{2,1,0:T(2,128)S(1)}, u32[]{:S(2)}, u32[]{:S(2)}) collective-permute-start(f32[12,2,32]{2,1,0:T(2,128)S(1)} %get-tuple-element.60), channel_id=1, source_target_pairs={{0,1},{1,2},{2,3},{3,4},{4,5},{5,6},{6,7},{7,8},{8,9},{9,10},{10,1... | collective-permute-start | bytes 9224 | tf_op jit(solution)/shard_map/ppermute | solution.py:25
  110.9 8.9 %collective-permute-start.16 = (f32[12,2,32]{2,1,0:T(2,128)S(1)}, f32[12,2,32]{2,1,0:T(2,128)S(1)}, u32[]{:S(2)}, u32[]{:S(2)}) collective-permute-start(f32[12,2,32]{2,1,0:T(2,128)S(1)} %get-tuple-element.61), channel_id=1, source_target_pairs={{1,0},{2,1},{3,2},{4,3},{5,4},{6,5},{7,6},{8,7},{9,8},{10,9},{11,1... | collective-permute-start | bytes 9224 | tf_op jit(solution)/shard_map/ppermute | solution.py:27
where the time goes:
time: 122 us; the launch traced here: 121 us
  starting transfers between devices  78.1 us (64%)
  waiting for transfers between devices  16.7 us (14%)
  other arithmetic  12.5 us (10%)
  local copies, waits for them, and re-layouts  11.6 us (10%)
  between operations  1.42 us (1%)
    ppermute x8, starting transfers between devices, extended(): lax.ppermute(head, axis, [((i + 1) % count, i) for i in range(ends)])  42.7 us
    ppermute x8, starting transfers between devices, extended(): lax.ppermute(tail, axis, [(i, (i + 1) % count) for i in range(ends)])  34.1 us
    ppermute x8, waiting for transfers between devices, extended(): lax.ppermute(head, axis, [((i + 1) % count, i) for i in range(ends)])  16.2 us
    eq x6, other arithmetic, pixel_fold(): (coords + displacement + offset) // 3 == home_pixel  3.99 us
    div x1, other arithmetic, body(): coefficient = COURANT / eps_cells  3.44 us
  transfers between devices with their start and end apart: 17, of which 6 were waited for; matrix products, arithmetic and copies ran while one was open for 12% of the time, Pallas kernels for 0%

commit v1 on v0

v1 whole, which is shorter than its diff:
```python
import math

import jax
import jax.numpy as jnp
from jax import lax
from jax.experimental import pallas as pl
from jax.experimental.pallas import tpu as pltpu
from jax.sharding import PartitionSpec as P

SLAB = 32
FREQ = 4
MATS = 4
COURANT = 0.5

BX, BY, CZ = 8, 16, 48
HY = BY // 2
LANES = 128
DEPTH = 2 * CZ
BOTTOM = CZ // 4
COMPS = 7
ROWS = COMPS * BX
PAIRS = BY // 2
SENT = 5
YY = 12
SUB = 16


def roll(v, by, axis):
    return pltpu.roll(v, by % v.shape[axis], axis)


def iota(shape, axis):
    return lax.broadcasted_iota(jnp.int32, shape, axis)


def third(v):
    return (v * 21846) >> 16


def same_pixel(coord, anchor, by):
    shifted = coord + anchor
    place = shifted - 3 * third(shifted) + by
    return (place >= 0) & (place <= 2)


def kernel(
    e_in, h_in, mat_in, perm, cells_in, amps_in, omegas, mask_in, fwd_in, anchor,
    adj, grad, fe,
    e_v, h_v, mat_v, cells_v, amps_v, mask_v, fwd_v, adj_v, coef_v,
    packed, edge, body, halo, merged, fields, source, flat,
    fe_send, fe_recv, g_send, g_x, g_y, g_c,
    load_sem, send_sem, recv_sem,
):
    nx, ny = lax.axis_size("gx"), lax.axis_size("gy")
    gx, gy, core = lax.axis_index("gx"), lax.axis_index("gy"), lax.axis_index("gz")
    other = 1 - core
    up_x, down_x = lax.rem(gx + 1, nx), lax.rem(gx + nx - 1, nx)
    up_y, down_y = lax.rem(gy + 1, ny), lax.rem(gy + ny - 1, ny)

    barrier = pltpu.get_barrier_semaphore()
    face_y = jnp.where(core == 0, down_y, up_y)
    senders = [(gx, gy, other)]
    for h in (0, 1):
        senders += [(up_x, gy, h), (down_x, gy, h)]
        senders += [(gx, face_y, h), (up_x, face_y, h), (down_x, face_y, h)]
    for sender in senders:
        pl.semaphore_signal(barrier, inc=1, device_id=sender, device_id_type=pl.DeviceIdType.MESH)

    loads = [
        pltpu.make_async_copy(src, dst, load_sem.at[i])
        for i, (src, dst) in enumerate(
            [(mat_in, mat_v), (e_in, e_v), (h_in, h_v), (cells_in, cells_v), (amps_in, amps_v),
             (mask_in, mask_v)]
            + [(fwd_in.at[:, pl.ds(LANES * t, LANES)], fwd_v.at[t]) for t in (0, 1)]
        )
    ]
    for load in loads:
        load.start()

    edge[...] = jnp.zeros_like(edge)
    halo[:, :, 16:48, :] = jnp.zeros((2, YY // 2, 32, LANES), jnp.float32)

    for load in loads[:3]:
        load.wait()
    material = mat_v[...]
    eps = jnp.zeros(material.shape, jnp.float32)
    for level in range(MATS):
        eps = eps + jnp.where(material == level, perm[level], 0.0)
    coef_v[...] = COURANT / eps
    blank = jnp.zeros((ROWS, LANES - DEPTH), jnp.float32)
    for pair in range(PAIRS):
        rows = [
            jnp.concatenate(
                [
                    e_v[pl.ds(y, 3 * BX, stride=BY), :],
                    h_v[pl.ds(y, 3 * BX, stride=BY), :],
                    coef_v[pl.ds(y, BX, stride=BY), :],
                ],
                axis=0,
            )
            for y in (2 * pair, 2 * pair + 1)
        ]
        packed[pair] = jnp.concatenate(rows + [blank], axis=1)
    for pair in range(PAIRS):
        for side, first in ((0, 0), (1, BX - 2)):
            for x in (0, 1):
                edge[side, pair, pl.ds(8 * x, COMPS), :] = packed[
                    pair, pl.ds(first + x, COMPS, stride=BX), :
                ]

    def remote(src, dst, role, device):
        return pltpu.make_async_remote_copy(
            src_ref=src,
            dst_ref=dst,
            send_sem=send_sem.at[role[0]],
            recv_sem=recv_sem.at[role[1]],
            device_id=device,
            device_id_type=pl.DeviceIdType.MESH,
        )

    def part(dest):
        return packed.at[pl.ds(3 * dest, SENT)]

    def part_edge(side, dest):
        return edge.at[side, pl.ds(3 * dest, SENT)]

    def span(dest):
        return pl.ds(1 - dest, SENT)

    pl.semaphore_wait(barrier, len(senders))
    sends = [
        remote(packed.at[PAIRS - 1], body.at[core, 0], (1, 1 + core), (gx, up_y, 0)),
        remote(packed.at[0], body.at[core, 5], (2, 1 + core), (gx, down_y, 1)),
    ]
    for side, to_x in ((0, down_x), (1, up_x)):
        place = pl.ds(48 * side, 16)
        sends += [
            remote(edge.at[side, PAIRS - 1], halo.at[core, 0, place], (3 + 4 * side, 7 + 2 * side + core), (to_x, up_y, 0)),
            remote(edge.at[side, 0], halo.at[core, 5, place], (4 + 4 * side, 7 + 2 * side + core), (to_x, down_y, 1)),
        ]
    for side, to_x in ((0, down_x), (1, up_x)):
        place = pl.ds(48 * side, 16)
        for dest in (0, 1):
            sends.append(
                remote(part_edge(side, dest), halo.at[core, span(dest), place], (5 + 4 * side + dest, 3 + 2 * side + core), (to_x, gy, dest))
            )
    sends.append(remote(part(other), body.at[core, span(other)], (0, 0), (gx, gy, other)))
    for send in sends:
        send.start()

    body[core, span(core)] = packed[pl.ds(3 * core, SENT)]
    for load in loads[3:]:
        load.wait()

    y_first = gy * BY + core * HY - 2
    row = iota((YY * SUB, 64), 0)
    sub = row & (SUB - 1)
    row_x = gx * BX + jnp.where(sub < 12, sub, sub - SUB)
    row_y = y_first + (row >> 4)
    hit = (row_x == cells_v[0:1, :]) & (row_y == cells_v[1:2, :])
    hit_z = jnp.where(iota((LANES, 64), 0) == cells_v[2:3, :], 1.0, 0.0)
    for c in range(3):
        left = jnp.where(hit, amps_v[c : c + 1, :], 0.0)
        source[c] = lax.dot_general(
            left, hit_z, (((1,), (1,)), ((), ())),
            precision=lax.Precision.HIGHEST, preferred_element_type=jnp.float32,
        ).reshape(YY, SUB, LANES)

    shape = (BX, LANES)
    r = iota(shape, 0)
    omega = jnp.zeros(shape, jnp.float32)
    for f in range(FREQ):
        omega = jnp.where((r & 3) == f, omegas[f], omega)
    phase = omega * ((r >> 2) + 1).astype(jnp.float32)
    cosine = jnp.cos(phase)
    sine = -jnp.sin(phase)
    square = omega * omega

    face = 1 - core
    y_in = jnp.where(core == 0, gy > 0, gy < ny - 1)

    remote(part(core), body.at[other, span(core)], (0, 0), (gx, gy, other)).wait_recv()
    for h in (0, 1):
        remote(packed.at[0], body.at[h, 5 * core], (0, 1 + h), (gx, gy, other)).wait_recv()
        for side in (0, 1):
            place = pl.ds(48 * side, 16)
            remote(edge.at[0, pl.ds(0, SENT)], halo.at[h, span(core), place], (0, 3 + 2 * side + h), (gx, gy, other)).wait_recv()
            remote(edge.at[0, 0], halo.at[h, 5 * core, place], (0, 7 + 2 * side + h), (gx, gy, other)).wait_recv()

    x_of = iota((SUB, LANES), 0)
    x_of = gx * BX + jnp.where(x_of < 12, x_of, x_of - SUB)
    lane = iota((SUB, LANES), 1)
    inside = (x_of >= 0) & (x_of < nx * BX) & (lane < DEPTH)
    y_end = ny * BY

    lane_b = iota((ROWS, LANES), 1)
    lane_h = iota((64, LANES), 1)

    def merge(low, high, lanes):
        even = jnp.where(lanes < CZ, low, roll(high, CZ, 1))
        odd = jnp.where(lanes < CZ, roll(low, -CZ, 1), high)
        return even, odd

    for pair in range(YY // 2):
        own = merge(body[0, pair], body[1, pair], lane_b)
        beside = merge(halo[0, pair], halo[1, pair], lane_h)
        for k in (0, 1):
            merged[k] = beside[k]
            yy = 2 * pair + k
            y = y_first + yy
            ok = inside & (y >= 0) & (y < y_end)
            for j in range(COMPS):
                tile = jnp.concatenate([own[k][BX * j : BX * j + BX], merged[k, pl.ds(j, 8, stride=8), :]], axis=0)
                fields[j, yy] = jnp.where(ok, tile, 0.0)

    half = jnp.where(inside, COURANT, 0.0)

    def magnetic_rows(first, last):
        def step(yy, carry):
            e0, e1, e2 = fields[0, yy], fields[1, yy], fields[2, yy]
            n0, n2 = fields[0, yy + 1], fields[2, yy + 1]
            y = y_first + yy
            scale = jnp.where((y >= 0) & (y < y_end), half, 0.0)
            fields[3, yy] = fields[3, yy] - scale * ((n2 - e2) - (roll(e1, -1, 1) - e1))
            fields[4, yy] = fields[4, yy] - scale * ((roll(e0, -1, 1) - e0) - (roll(e2, -1, 0) - e2))
            fields[5, yy] = fields[5, yy] - scale * ((roll(e1, -1, 0) - e1) - (n0 - e0))
            return carry

        lax.fori_loop(first, last, step, 0, unroll=True)

    def electric_rows(first, last, time):
        factor = math.cos(0.7 * (time + 0.5))

        def step(yy, carry):
            h0, h1, h2 = fields[3, yy], fields[4, yy], fields[5, yy]
            p0, p2 = fields[3, yy - 1], fields[5, yy - 1]
            scale = fields[6, yy]
            curls = (
                (h2 - p2) - (h1 - roll(h1, 1, 1)),
                (h0 - roll(h0, 1, 1)) - (h2 - roll(h2, 1, 0)),
                (h1 - roll(h1, 1, 0)) - (h0 - p0),
            )
            for c in range(3):
                fields[c, yy] = fields[c, yy] + scale * (curls[c] - factor * source[c, yy])
            return carry

        lax.fori_loop(first, last, step, 0, unroll=True)

    quarter = iota((BX, LANES), 1) >> 5

    def flatten(time):
        for c in range(3):
            for tile in (0, 1):
                out = jnp.zeros((BX, LANES), jnp.float32)
                for q in range(4):
                    v = fields[c, 2 + 4 * tile + q, 0:BX, :]
                    out = jnp.where(quarter == q, roll(v, SLAB * q - BOTTOM, 1), out)
                flat[time, c, :, pl.ds(LANES * tile, LANES)] = out

    magnetic_rows(0, 11)
    electric_rows(1, 11, 0)
    flatten(0)
    magnetic_rows(1, 10)
    electric_rows(2, 10, 1)
    flatten(1)

    for y in range(HY):
        v = jnp.concatenate([fields[c, 2 + y, 0:BX, :] for c in range(3)], axis=0)
        moved = roll(v, -CZ, 1)
        first = core == 0
        fe[pl.ds(HY * core + y, 3 * BX, stride=BY), :] = jnp.where(first, v, moved)[:, :CZ]
        fe_send[y] = jnp.where(first, moved, v)
    fe_copy = remote(fe_send, fe_recv, (11, 11), (gx, gy, other))
    fe_copy.start()

    totals = []
    for t in (0, 1):
        lanes = pl.ds(LANES * t, LANES)
        total = jnp.zeros((BX, LANES), jnp.float32)
        for f in range(FREQ):
            real = jnp.zeros((BX, LANES), jnp.float32)
            for p, weights in ((0, cosine), (1, sine)):
                for c in range(3):
                    rows = pl.ds(3 * FREQ * p + 3 * f + c, BX, stride=6 * FREQ)
                    value = weights[f : f + 1, :] * flat[0, c, :, lanes] + weights[4 + f : 5 + f, :] * flat[1, c, :, lanes]
                    adj_v[t, rows, :] = value
                    product = fwd_v[t, rows, :] * value
                    real = real + product if p == 0 else real - product
            total = total + square[f : f + 1, :] * real
        totals.append(total)
    stores = [
        pltpu.make_async_copy(adj_v.at[t], adj.at[:, pl.ds(LANES * t, LANES)], load_sem.at[8 + t]) for t in (0, 1)
    ]
    for store in stores:
        store.start()
    total = 0.05 * jnp.concatenate(totals, axis=1) * mask_v[...].astype(jnp.float32)

    shape = (BX, 2 * LANES)
    z = iota(shape, 1) & (SLAB - 1)
    folded = total
    for by in (-2, -1, 1, 2):
        ok = same_pixel(z, anchor[2], by) & (z + by >= 0) & (z + by < SLAB)
        folded = folded + jnp.where(ok, roll(total, -by, 1), 0.0)
    g_send[...] = folded

    above = (gx, jnp.where(core == 0, gy, up_y), other)
    below = (gx, jnp.where(core == 0, down_y, gy), other)
    first_rows, last_rows = g_send.at[:, pl.ds(0, LANES)], g_send.at[:, pl.ds(LANES, LANES)]
    swaps = [
        remote(first_rows, g_y.at[0], (12, 12), below),
        remote(last_rows, g_y.at[1], (13, 13), above),
        remote(first_rows, g_c.at[0, 0], (14, 14), (down_x,) + below[1:]),
        remote(last_rows, g_c.at[0, 1], (15, 15), (down_x,) + above[1:]),
        remote(first_rows, g_c.at[1, 0], (16, 16), (up_x,) + below[1:]),
        remote(last_rows, g_c.at[1, 1], (17, 17), (up_x,) + above[1:]),
        remote(g_send, g_x.at[0], (18, 18), (down_x, gy, core)),
        remote(g_send, g_x.at[1], (19, 19), (up_x, gy, core)),
    ]
    for swap in swaps:
        swap.start()

    fe_copy.wait_recv()
    for y in range(HY):
        fe[pl.ds(HY * other + y, 3 * BX, stride=BY), :] = fe_recv[y][:, :CZ]

    for swap in swaps:
        swap.wait_recv()
    block = gy * 2 + core
    wide = (BX, 4 * LANES)
    tile0 = jnp.concatenate([folded, g_y[0], g_y[1]], axis=1)
    upper = jnp.concatenate([g_x[0], g_c[0, 0], g_c[0, 1]], axis=1)
    lower = jnp.concatenate([g_x[1], g_c[1, 0], g_c[1, 1]], axis=1)
    x_row, column = iota(wide, 0), iota(wide, 1)
    upper = jnp.where(gx < nx - 1, upper, 0.0)
    lower = jnp.where(gx > 0, lower, 0.0)
    tile1 = jnp.where(x_row < 4, upper, lower)
    y_ok = (column < 2 * LANES) | ((column < 3 * LANES) & (block < 2 * ny - 1)) | ((column >= 3 * LANES) & (block > 0))
    extended = jnp.where(
        jnp.concatenate([y_ok, y_ok], axis=0), jnp.concatenate([tile0, tile1], axis=0), 0.0
    )
    along_x = extended[:BX]
    for by in (-2, -1, 1, 2):
        ok = same_pixel(gx * BX + x_row, anchor[0], by)
        along_x = along_x + jnp.where(ok, roll(extended, -by, 0)[:BX], 0.0)
    result = along_x[:, : 2 * LANES]
    y_row = block * HY + (iota(shape, 1) >> 5)
    for by in (-2, -1, 1, 2):
        ok = same_pixel(y_row, anchor[1], by)
        result = result + jnp.where(ok, roll(along_x, -SLAB * by, 1)[:, : 2 * LANES], 0.0)
    grad[...] = result

    for send in sends + [fe_copy] + swaps:
        send.wait_send()
    for store in stores:
        store.wait()


def body_fn(
    electric, magnetic, material, permittivity, source_cells, amplitudes, omegas, design_mask, forward_dft, pixel_anchor
):
    f32 = jnp.float32
    anywhere = pl.BlockSpec(memory_space=pl.ANY)
    scalars = pl.BlockSpec(memory_space=pltpu.SMEM)
    vmem = pl.BlockSpec(memory_space=pltpu.VMEM)
    adj, grad, fe = pl.pallas_call(
        kernel,
        out_shape=(
            jax.ShapeDtypeStruct((BX * 6 * FREQ, 2 * LANES), f32),
            jax.ShapeDtypeStruct((BX, 2 * LANES), f32),
            jax.ShapeDtypeStruct((3 * BX * BY, CZ), f32),
        ),
        in_specs=[anywhere, anywhere, anywhere, scalars, anywhere, anywhere, scalars, anywhere, anywhere, scalars],
        out_specs=(anywhere, vmem, vmem),
        scratch_shapes=[
            pltpu.VMEM((3 * BX * BY, CZ), f32),
            pltpu.VMEM((3 * BX * BY, CZ), f32),
            pltpu.VMEM((BX * BY, CZ), jnp.int32),
            pltpu.VMEM((3, 64), jnp.int32),
            pltpu.VMEM((3, 64), f32),
            pltpu.VMEM((BX, 2 * LANES), jnp.int32),
            pltpu.VMEM((2, BX * 6 * FREQ, LANES), f32),
            pltpu.VMEM((2, BX * 6 * FREQ, LANES), f32),
            pltpu.VMEM((BX * BY, CZ), f32),
            pltpu.VMEM((PAIRS, ROWS, LANES), f32),
            pltpu.VMEM((2, PAIRS, 16, LANES), f32),
            pltpu.VMEM((2, YY // 2, ROWS, LANES), f32),
            pltpu.VMEM((2, YY // 2, 64, LANES), f32),
            pltpu.VMEM((2, 64, LANES), f32),
            pltpu.VMEM((COMPS, YY, SUB, LANES), f32),
            pltpu.VMEM((3, YY, SUB, LANES), f32),
            pltpu.VMEM((2, 3, BX, 2 * LANES), f32),
            pltpu.VMEM((HY, 3 * BX, LANES), f32),
            pltpu.VMEM((HY, 3 * BX, LANES), f32),
            pltpu.VMEM((BX, 2 * LANES), f32),
            pltpu.VMEM((2, BX, 2 * LANES), f32),
            pltpu.VMEM((2, BX, LANES), f32),
            pltpu.VMEM((2, 2, BX, LANES), f32),
            pltpu.SemaphoreType.DMA((10,)),
            pltpu.SemaphoreType.DMA((20,)),
            pltpu.SemaphoreType.DMA((20,)),
        ],
        compiler_params=pltpu.CompilerParams(
            collective_id=0, has_side_effects=True, vmem_limit_bytes=24 * 1024 * 1024
        ),
    )(
        electric.reshape(3 * BX * BY, CZ),
        magnetic.reshape(3 * BX * BY, CZ),
        material.reshape(BX * BY, CZ),
        permittivity,
        source_cells.T,
        amplitudes.T,
        omegas,
        design_mask,
        forward_dft.reshape(BX * 6 * FREQ, 2 * LANES),
        pixel_anchor,
    )
    return adj.reshape(BX, 6 * FREQ, 2 * LANES), grad, fe.reshape(3, BX, BY, CZ)


def solution(mesh):
    return jax.shard_map(
        body_fn,
        mesh=mesh,
        in_specs=(
            P(None, "gx", "gy", "gz"),
            P(None, "gx", "gy", "gz"),
            P("gx", "gy", "gz"),
            P(),
            P(),
            P(),
            P(),
            P("gx", ("gy", "gz")),
            P("gx", None, ("gy", "gz")),
            P(),
        ),
        out_specs=(P("gx", None, ("gy", "gz")), P("gx", ("gy", "gz")), P(None, "gx", "gy", "gz")),
        check_vma=False,
    )
```

time: 122 us -> 46.6 us (0.38)
  the two profiles are of different devices: /device:TPU:23 before, /device:TPU:1 now
where the time goes in v1:
time: 46.6 us; the launch traced here: 45.8 us
  Pallas kernels  37.6 us (81%)
  local copies, waits for them, and re-layouts  7.58 us (16%)
  between operations  0.69 us (1%)
    pallas_call x1, Pallas kernels, body_fn(): pl.pallas_call(kernel, out_shape=(jax.ShapeDtypeStruct((BX * 6 * FREQ, 2...  37.6 us
    unnamed x23, local copies, waits for them, and re-layouts  7.58 us

profile of v1, /device:TPU:1, one launch (start us, length us, event | category | flops | bytes accessed | tf_op | source)
XLA Modules:
  0.0 45.8 jit_solution(8431424046484446855)
XLA Ops:
  0.6 0.0 copy-start.4
  0.6 0.0 copy-start.5
  0.7 0.0 copy-start.7
  0.7 0.0 copy-start.8
  0.7 0.7 %copy-done.4 = s32[8,256]{1,0:T(8,128)S(1)} copy-done((s32[8,256]{1,0:T(8,128)S(1)}, s32[8,256]{1,0:T(8,128)}, u32[]{:S(2)}) %copy-start.4) | copy-done | bytes 8216
  1.3 0.0 copy-done.5
  1.3 0.0 copy-done.7
  1.3 0.0 copy-done.8
  1.3 0.0 copy-start
  1.3 0.9 %copy-done = f32[3,8,16,48]{3,2,1,0:T(8,128)S(1)} copy-done((f32[3,8,16,48]{3,2,1,0:T(8,128)S(1)}, f32[3,8,16,48]{3,2,1,0:T(8,128)}, u32[]{:S(2)}) %copy-start) | copy-done | bytes 73752
  2.3 0.0 copy-start.1
  2.3 0.9 %copy-done.1 = f32[3,8,16,48]{3,2,1,0:T(8,128)S(1)} copy-done((f32[3,8,16,48]{3,2,1,0:T(8,128)S(1)}, f32[3,8,16,48]{3,2,1,0:T(8,128)}, u32[]{:S(2)}) %copy-start.1) | copy-done | bytes 73752
  3.2 0.0 copy-start.2
  3.2 0.9 %copy-done.2 = f32[8,24,256]{2,1,0:T(8,128)S(1)} copy-done((f32[8,24,256]{2,1,0:T(8,128)S(1)}, f32[8,24,256]{2,1,0:T(8,128)}, u32[]{:S(2)}) %copy-start.2) | copy-done | bytes 196632
  4.1 0.0 copy-start.3
  4.1 0.8 %copy-done.3 = s32[8,16,48]{2,1,0:T(8,128)S(1)} copy-done((s32[8,16,48]{2,1,0:T(8,128)S(1)}, s32[8,16,48]{2,1,0:T(8,128)}, u32[]{:S(2)}) %copy-start.3) | copy-done | bytes 24600
  5.0 0.0 copy-start.6
  5.0 0.7 %copy-done.6 = f32[64,3]{0,1:T(4,128)S(1)} copy-done((f32[64,3]{0,1:T(4,128)S(1)}, f32[64,3]{0,1:T(4,128)}, u32[]{:S(2)}) %copy-start.6) | copy-done | bytes 792
  5.6 0.0 copy-start.9
  5.6 0.7 %copy-done.9 = s32[3]{0:T(128)S(1)} copy-done((s32[3]{0:T(128)S(1)}, s32[3]{0:T(128)}, u32[]{:S(2)}) %copy-start.9) | copy-done | bytes 36
  6.3 37.6 %shard_map.121 = (f32[192,256]{1,0:T(8,128)S(1)}, f32[8,256]{1,0:T(8,128)S(1)}, f32[384,48]{1,0:T(8,128)S(1)}) custom-call(f32[384,48]{1,0:T(8,128)S(1)} %bitcast.10, f32[384,48]{1,0:T(8,128)S(1)} %bitcast.11, s32[128,48]{1,0:T(8,128)S(1)} %bitcast.13, f32[4]{0:T(128)S(1)} %copy-done.7, s32[3,64]{1,0:T(4,128)S(1)} %bitcast.14, f32[3,64]{1,0:T(4,128)S(1)} %bitcast.15, ...), custom_call_target="tpu_custom_call" | custom-call | tf_op jit(solution)/shard_map/pallas_call | solution.py:365
  43.9 0.7 %copy.16 = f32[8,24,256]{2,1,0:T(8,128)} copy(f32[8,24,256]{2,1,0:T(8,128)S(1)} %bitcast.9) | data formatting | bytes 393216
  44.6 0.6 %copy.17 = f32[8,256]{1,0:T(8,128)} copy(f32[8,256]{1,0:T(8,128)S(1)} %get-tuple-element.13) | data formatting | bytes 16384
  45.2 0.7 %copy.18 = f32[3,8,16,48]{3,2,1,0:T(8,128)} copy(f32[3,8,16,48]{3,2,1,0:T(8,128)S(1)} %bitcast.8) | data formatting | bytes 147456
Async XLA Ops:
  0.6 0.7 %copy-start.4 = (s32[8,256]{1,0:T(8,128)S(1)}, s32[8,256]{1,0:T(8,128)}, u32[]{:S(2)}) copy-start(s32[8,256]{1,0:T(8,128)} %mask_in.1) | copy-start | bytes 24580
  0.6 0.7 %copy-start.5 = (s32[64,3]{0,1:T(4,128)S(1)}, s32[64,3]{0,1:T(4,128)}, u32[]{:S(2)}) copy-start(s32[64,3]{0,1:T(4,128)} %param.14) | copy-start | bytes 2308
  0.7 0.7 %copy-start.7 = (f32[4]{0:T(128)S(1)}, f32[4]{0:T(128)}, u32[]{:S(2)}) copy-start(f32[4]{0:T(128)} %perm.1) | copy-start | bytes 52
  0.7 0.7 %copy-start.8 = (f32[4]{0:T(128)S(1)}, f32[4]{0:T(128)}, u32[]{:S(2)}) copy-start(f32[4]{0:T(128)} %omegas.1) | copy-start | bytes 52
  1.3 0.9 %copy-start = (f32[3,8,16,48]{3,2,1,0:T(8,128)S(1)}, f32[3,8,16,48]{3,2,1,0:T(8,128)}, u32[]{:S(2)}) copy-start(f32[3,8,16,48]{3,2,1,0:T(8,128)} %param.10) | copy-start | bytes 221188
  2.3 0.9 %copy-start.1 = (f32[3,8,16,48]{3,2,1,0:T(8,128)S(1)}, f32[3,8,16,48]{3,2,1,0:T(8,128)}, u32[]{:S(2)}) copy-start(f32[3,8,16,48]{3,2,1,0:T(8,128)} %param.11) | copy-start | bytes 221188
  3.2 0.9 %copy-start.2 = (f32[8,24,256]{2,1,0:T(8,128)S(1)}, f32[8,24,256]{2,1,0:T(8,128)}, u32[]{:S(2)}) copy-start(f32[8,24,256]{2,1,0:T(8,128)} %param.18) | copy-start | bytes 589828
  4.1 0.8 %copy-start.3 = (s32[8,16,48]{2,1,0:T(8,128)S(1)}, s32[8,16,48]{2,1,0:T(8,128)}, u32[]{:S(2)}) copy-start(s32[8,16,48]{2,1,0:T(8,128)} %param.12) | copy-start | bytes 73732
  5.0 0.7 %copy-start.6 = (f32[64,3]{0,1:T(4,128)S(1)}, f32[64,3]{0,1:T(4,128)}, u32[]{:S(2)}) copy-start(f32[64,3]{0,1:T(4,128)} %param.15) | copy-start | bytes 2308
  5.6 0.7 %copy-start.9 = (s32[3]{0:T(128)S(1)}, s32[3]{0:T(128)}, u32[]{:S(2)}) copy-start(s32[3]{0:T(128)} %anchor.1) | copy-start | bytes 40

commit v2 on v1

--- a/solution.py
+++ b/solution.py
@@ -44,10 +44,11 @@
 
 
 def kernel(
-    e_in, h_in, mat_in, perm, cells_in, amps_in, omegas, mask_in, fwd_in, anchor,
+    e_in, h_in, mat_in, perm_in, cells_in, amps_in, omegas_in, mask_in, fwd_in, anchor_in,
     adj, grad, fe,
+    perm, omegas, anchor,
     e_v, h_v, mat_v, cells_v, amps_v, mask_v, fwd_v, adj_v, coef_v,
-    packed, edge, body, halo, merged, fields, source, flat,
+    packed, edge, body, halo, merged, fields, source, gain, flat,
     fe_send, fe_recv, g_send, g_x, g_y, g_c,
     load_sem, send_sem, recv_sem,
 ):
@@ -69,8 +70,8 @@
     loads = [
         pltpu.make_async_copy(src, dst, load_sem.at[i])
         for i, (src, dst) in enumerate(
-            [(mat_in, mat_v), (e_in, e_v), (h_in, h_v), (cells_in, cells_v), (amps_in, amps_v),
-             (mask_in, mask_v)]
+            [(perm_in, perm), (mat_in, mat_v), (e_in, e_v), (h_in, h_v), (cells_in, cells_v), (amps_in, amps_v),
+             (omegas_in, omegas), (anchor_in, anchor), (mask_in, mask_v)]
             + [(fwd_in.at[:, pl.ds(LANES * t, LANES)], fwd_v.at[t]) for t in (0, 1)]
         )
     ]
@@ -80,7 +81,7 @@
     edge[...] = jnp.zeros_like(edge)
     halo[:, :, 16:48, :] = jnp.zeros((2, YY // 2, 32, LANES), jnp.float32)
 
-    for load in loads[:3]:
+    for load in loads[:4]:
         load.wait()
     material = mat_v[...]
     eps = jnp.zeros(material.shape, jnp.float32)
@@ -149,7 +150,7 @@
         send.start()
 
     body[core, span(core)] = packed[pl.ds(3 * core, SENT)]
-    for load in loads[3:]:
+    for load in loads[4:]:
         load.wait()
 
     y_first = gy * BY + core * HY - 2
@@ -176,8 +177,19 @@
     sine = -jnp.sin(phase)
     square = omega * omega
 
-    face = 1 - core
-    y_in = jnp.where(core == 0, gy > 0, gy < ny - 1)
+    for t in (0, 1):
+        lanes = pl.ds(LANES * t, LANES)
+        design = 0.05 * mask_v[:, lanes].astype(jnp.float32)
+        for c in range(3):
+            gains = [jnp.zeros((BX, LANES), jnp.float32)] * 2
+            for f in range(FREQ):
+                real = square[f : f + 1, :] * fwd_v[t, pl.ds(3 * f + c, BX, stride=6 * FREQ), :]
+                imag = square[f : f + 1, :] * fwd_v[t, pl.ds(3 * FREQ + 3 * f + c, BX, stride=6 * FREQ), :]
+                for n in (0, 1):
+                    k = FREQ * n + f
+                    gains[n] = gains[n] + cosine[k : k + 1, :] * real - sine[k : k + 1, :] * imag
+            for n in (0, 1):
+                gain[n, c, :, lanes] = design * gains[n]
 
     remote(part(core), body.at[other, span(core)], (0, 0), (gx, gy, other)).wait_recv()
     for h in (0, 1):
@@ -264,38 +276,12 @@
     electric_rows(2, 10, 1)
     flatten(1)
 
-    for y in range(HY):
-        v = jnp.concatenate([fields[c, 2 + y, 0:BX, :] for c in range(3)], axis=0)
-        moved = roll(v, -CZ, 1)
-        first = core == 0
-        fe[pl.ds(HY * core + y, 3 * BX, stride=BY), :] = jnp.where(first, v, moved)[:, :CZ]
-        fe_send[y] = jnp.where(first, moved, v)
-    fe_copy = remote(fe_send, fe_recv, (11, 11), (gx, gy, other))
-    fe_copy.start()
-
-    totals = []
-    for t in (0, 1):
-        lanes = pl.ds(LANES * t, LANES)
-        total = jnp.zeros((BX, LANES), jnp.float32)
-        for f in range(FREQ):
-            real = jnp.zeros((BX, LANES), jnp.float32)
-            for p, weights in ((0, cosine), (1, sine)):
-                for c in range(3):
-                    rows = pl.ds(3 * FREQ * p + 3 * f + c, BX, stride=6 * FREQ)
-                    value = weights[f : f + 1, :] * flat[0, c, :, lanes] + weights[4 + f : 5 + f, :] * flat[1, c, :, lanes]
-                    adj_v[t, rows, :] = value
-                    product = fwd_v[t, rows, :] * value
-                    real = real + product if p == 0 else real - product
-            total = total + square[f : f + 1, :] * real
-        totals.append(total)
-    stores = [
-        pltpu.make_async_copy(adj_v.at[t], adj.at[:, pl.ds(LANES * t, LANES)], load_sem.at[8 + t]) for t in (0, 1)
-    ]
-    for store in stores:
-        store.start()
-    total = 0.05 * jnp.concatenate(totals, axis=1) * mask_v[...].astype(jnp.float32)
-
     shape = (BX, 2 * LANES)
+    total = jnp.zeros(shape, jnp.float32)
+    for n in (0, 1):
+        for c in range(3):
+            total = total + gain[n, c] * flat[n, c]
+
     z = iota(shape, 1) & (SLAB - 1)
     folded = total
     for by in (-2, -1, 1, 2):
@@ -318,6 +304,31 @@
     ]
     for swap in swaps:
         swap.start()
+
+    for y in range(HY):
+        v = jnp.concatenate([fields[c, 2 + y, 0:BX, :] for c in range(3)], axis=0)
+        moved = roll(v, -CZ, 1)
+        first = core == 0
+        fe[pl.ds(HY * core + y, 3 * BX, stride=BY), :] = jnp.where(first, v, moved)[:, :CZ]
+        fe_send[y] = jnp.where(first, moved, v)
+    fe_copy = remote(fe_send, fe_recv, (11, 11), (gx, gy, other))
+    fe_copy.start()
+
+    for t in (0, 1):
+        lanes = pl.ds(LANES * t, LANES)
+        for f in range(FREQ):
+            for p, weights in ((0, cosine), (1, sine)):
+                for c in range(3):
+                    rows = pl.ds(3 * FREQ * p + 3 * f + c, BX, stride=6 * FREQ)
+                    adj_v[t, rows, :] = (
+                        weights[f : f + 1, :] * flat[0, c, :, lanes]
+                        + weights[FREQ + f : FREQ + f + 1, :] * flat[1, c, :, lanes]
+                    )
+    stores = [
+        pltpu.make_async_copy(adj_v.at[t], adj.at[:, pl.ds(LANES * t, LANES)], load_sem.at[11 + t]) for t in (0, 1)
+    ]
+    for store in stores:
+        store.start()
 
     fe_copy.wait_recv()
     for y in range(HY):
@@ -355,12 +366,22 @@
         store.wait()
 
 
+def deliver(adj, grad, fe, adj_out, grad_out, fe_out, sem):
+    copies = [
+        pltpu.make_async_copy(src, dst, sem.at[i])
+        for i, (src, dst) in enumerate([(adj, adj_out), (fe, fe_out), (grad, grad_out)])
+    ]
+    for copy in copies:
+        copy.start()
+    for copy in copies:
+        copy.wait()
+
+
 def body_fn(
     electric, magnetic, material, permittivity, source_cells, amplitudes, omegas, design_mask, forward_dft, pixel_anchor
 ):
     f32 = jnp.float32
     anywhere = pl.BlockSpec(memory_space=pl.ANY)
-    scalars = pl.BlockSpec(memory_space=pltpu.SMEM)
     vmem = pl.BlockSpec(memory_space=pltpu.VMEM)
     adj, grad, fe = pl.pallas_call(
         kernel,
@@ -369,9 +390,12 @@
             jax.ShapeDtypeStruct((BX, 2 * LANES), f32),
             jax.ShapeDtypeStruct((3 * BX * BY, CZ), f32),
         ),
-        in_specs=[anywhere, anywhere, anywhere, scalars, anywhere, anywhere, scalars, anywhere, anywhere, scalars],
+        in_specs=[anywhere] * 10,
         out_specs=(anywhere, vmem, vmem),
         scratch_shapes=[
+            pltpu.SMEM((MATS,), f32),
+            pltpu.SMEM((FREQ,), f32),
+            pltpu.SMEM((3,), jnp.int32),
             pltpu.VMEM((3 * BX * BY, CZ), f32),
             pltpu.VMEM((3 * BX * BY, CZ), f32),
             pltpu.VMEM((BX * BY, CZ), jnp.int32),
@@ -389,13 +413,14 @@
             pltpu.VMEM((COMPS, YY, SUB, LANES), f32),
             pltpu.VMEM((3, YY, SUB, LANES), f32),
             pltpu.VMEM((2, 3, BX, 2 * LANES), f32),
+            pltpu.VMEM((2, 3, BX, 2 * LANES), f32),
             pltpu.VMEM((HY, 3 * BX, LANES), f32),
             pltpu.VMEM((HY, 3 * BX, LANES), f32),
             pltpu.VMEM((BX, 2 * LANES), f32),
             pltpu.VMEM((2, BX, 2 * LANES), f32),
             pltpu.VMEM((2, BX, LANES), f32),
             pltpu.VMEM((2, 2, BX, LANES), f32),
-            pltpu.SemaphoreType.DMA((10,)),
+            pltpu.SemaphoreType.DMA((13,)),
             pltpu.SemaphoreType.DMA((20,)),
             pltpu.SemaphoreType.DMA((20,)),
         ],
@@ -403,17 +428,30 @@
             collective_id=0, has_side_effects=True, vmem_limit_bytes=24 * 1024 * 1024
         ),
     )(
-        electric.reshape(3 * BX * BY, CZ),
-        magnetic.reshape(3 * BX * BY, CZ),
-        material.reshape(BX * BY, CZ),
-        permittivity,
-        source_cells.T,
-        amplitudes.T,
-        omegas,
-        design_mask,
-        forward_dft.reshape(BX * 6 * FREQ, 2 * LANES),
-        pixel_anchor,
+        *[
+            pltpu.with_memory_space_constraint(v, pltpu.HBM)
+            for v in (
+                electric.reshape(3 * BX * BY, CZ),
+                magnetic.reshape(3 * BX * BY, CZ),
+                material.reshape(BX * BY, CZ),
+                permittivity,
+                source_cells.T,
+                amplitudes.T,
+                omegas,
+                design_mask,
+                forward_dft.reshape(BX * 6 * FREQ, 2 * LANES),
+                pixel_anchor,
+            )
+        ]
     )
+    adj, grad, fe = pl.pallas_call(
+        deliver,
+        out_shape=tuple(jax.ShapeDtypeStruct(v.shape, f32) for v in (adj, grad, fe)),
+        in_specs=[anywhere] * 3,
+        out_specs=(anywhere,) * 3,
+        scratch_shapes=[pltpu.SemaphoreType.DMA((3,))],
+        compiler_params=pltpu.CompilerParams(vmem_limit_bytes=1024 * 1024),
+    )(adj, grad, fe)
     return adj.reshape(BX, 6 * FREQ, 2 * LANES), grad, fe.reshape(3, BX, BY, CZ)
 
 

time: 46.6 us -> 39 us (0.84)
  local copies, waits for them, and re-layouts: 7.58 us -> 0 us
    unnamed x23 -> x0, local copies, waits for them, and re-layouts: 7.58 us -> none
    pallas_call x0 -> x1, Pallas kernels: none -> 0.77 us  [body_fn(): pl.pallas_call(deliver, out_shape=tuple((jax.ShapeDtypeStruct(v.shape, f3...]
    pallas_call x1, Pallas kernels: 37.6 us -> 37 us  [body_fn(): pl.pallas_call(kernel, out_shape=(jax.ShapeDtypeStruct((BX * 6 * FREQ, 2...]
where the time goes in v2:
time: 39 us; the launch traced here: 38.4 us
  Pallas kernels  37.7 us (97%)
  between operations  0.64 us (2%)
    pallas_call x1, Pallas kernels, body_fn(): pl.pallas_call(kernel, out_shape=(jax.ShapeDtypeStruct((BX * 6 * FREQ, 2...  37 us

profile of v2, /device:TPU:1, one launch (start us, length us, event | category | flops | bytes accessed | tf_op | source)
XLA Modules:
  0.0 38.4 jit_solution(18256101303946536303)
XLA Ops:
  0.6 37.0 %shard_map.121 = (f32[192,256]{1,0:T(8,128)S(1)}, f32[8,256]{1,0:T(8,128)S(1)}, f32[384,48]{1,0:T(8,128)S(1)}) custom-call(f32[384,48]{1,0:T(8,128)} %bitcast.8, f32[384,48]{1,0:T(8,128)} %bitcast.9, s32[128,48]{1,0:T(8,128)} %bitcast.11, f32[4]{0:T(128)} %perm_in.1, s32[3,64]{1,0:T(4,128)} %bitcast.12, f32[3,64]{1,0:T(4,128)} %bitcast.13, f32[4]{0:T(128)} %omegas_in.1, ...), custom_call_target="tpu_custom_call" | custom-call | tf_op jit(solution)/shard_map/pallas_call | solution.py:386
  37.6 0.8 %shard_map.122 = (f32[192,256]{1,0:T(8,128)}, f32[8,256]{1,0:T(8,128)}, f32[384,48]{1,0:T(8,128)}) custom-call(f32[192,256]{1,0:T(8,128)S(1)} %get-tuple-element.9.adj, f32[8,256]{1,0:T(8,128)S(1)} %get-tuple-element.10.grad, f32[384,48]{1,0:T(8,128)S(1)} %get-tuple-element.11.fe), custom_call_target="tpu_custom_call" | custom-call | tf_op jit(solution)/shard_map/pallas_call | solution.py:447

commit v3 on v2

--- a/solution.py
+++ b/solution.py
@@ -20,9 +20,9 @@
 COMPS = 7
 ROWS = COMPS * BX
 PAIRS = BY // 2
-SENT = 5
-YY = 12
-SUB = 16
+WIDE = 4
+YY = HY + 2 * WIDE
+SUB = BX + 2 * WIDE
 
 
 def roll(v, by, axis):
@@ -48,8 +48,8 @@
     adj, grad, fe,
     perm, omegas, anchor,
     e_v, h_v, mat_v, cells_v, amps_v, mask_v, fwd_v, adj_v, coef_v,
-    packed, edge, body, halo, merged, fields, source, gain, flat,
-    fe_send, fe_recv, g_send, g_x, g_y, g_c,
+    packed, edge, body0, body1, halo0, halo1, merged, fields, source, gain, flat,
+    fe_send, fe_recv, sx, sy, sc, g_x, g_y, g_c,
     load_sem, send_sem, recv_sem,
 ):
     nx, ny = lax.axis_size("gx"), lax.axis_size("gy")
@@ -79,7 +79,7 @@
         load.start()
 
     edge[...] = jnp.zeros_like(edge)
-    halo[:, :, 16:48, :] = jnp.zeros((2, YY // 2, 32, LANES), jnp.float32)
+    halo1[:, 16:48, :] = jnp.zeros((PAIRS - 2, 32, LANES), jnp.float32)
 
     for load in loads[:4]:
         load.wait()
@@ -103,69 +103,11 @@
         ]
         packed[pair] = jnp.concatenate(rows + [blank], axis=1)
     for pair in range(PAIRS):
-        for side, first in ((0, 0), (1, BX - 2)):
-            for x in (0, 1):
-                edge[side, pair, pl.ds(8 * x, COMPS), :] = packed[
-                    pair, pl.ds(first + x, COMPS, stride=BX), :
-                ]
-
-    def remote(src, dst, role, device):
-        return pltpu.make_async_remote_copy(
-            src_ref=src,
-            dst_ref=dst,
-            send_sem=send_sem.at[role[0]],
-            recv_sem=recv_sem.at[role[1]],
-            device_id=device,
-            device_id_type=pl.DeviceIdType.MESH,
-        )
-
-    def part(dest):
-        return packed.at[pl.ds(3 * dest, SENT)]
-
-    def part_edge(side, dest):
-        return edge.at[side, pl.ds(3 * dest, SENT)]
-
-    def span(dest):
-        return pl.ds(1 - dest, SENT)
-
-    pl.semaphore_wait(barrier, len(senders))
-    sends = [
-        remote(packed.at[PAIRS - 1], body.at[core, 0], (1, 1 + core), (gx, up_y, 0)),
-        remote(packed.at[0], body.at[core, 5], (2, 1 + core), (gx, down_y, 1)),
-    ]
-    for side, to_x in ((0, down_x), (1, up_x)):
-        place = pl.ds(48 * side, 16)
-        sends += [
-            remote(edge.at[side, PAIRS - 1], halo.at[core, 0, place], (3 + 4 * side, 7 + 2 * side + core), (to_x, up_y, 0)),
-            remote(edge.at[side, 0], halo.at[core, 5, place], (4 + 4 * side, 7 + 2 * side + core), (to_x, down_y, 1)),
-        ]
-    for side, to_x in ((0, down_x), (1, up_x)):
-        place = pl.ds(48 * side, 16)
-        for dest in (0, 1):
-            sends.append(
-                remote(part_edge(side, dest), halo.at[core, span(dest), place], (5 + 4 * side + dest, 3 + 2 * side + core), (to_x, gy, dest))
-            )
-    sends.append(remote(part(other), body.at[core, span(other)], (0, 0), (gx, gy, other)))
-    for send in sends:
-        send.start()
-
-    body[core, span(core)] = packed[pl.ds(3 * core, SENT)]
+        for side in (0, 1):
+            for x in range(WIDE):
+                edge[side, pair, pl.ds(8 * x, COMPS), :] = packed[pair, pl.ds(WIDE * side + x, COMPS, stride=BX), :]
     for load in loads[4:]:
         load.wait()
-
-    y_first = gy * BY + core * HY - 2
-    row = iota((YY * SUB, 64), 0)
-    sub = row & (SUB - 1)
-    row_x = gx * BX + jnp.where(sub < 12, sub, sub - SUB)
-    row_y = y_first + (row >> 4)
-    hit = (row_x == cells_v[0:1, :]) & (row_y == cells_v[1:2, :])
-    hit_z = jnp.where(iota((LANES, 64), 0) == cells_v[2:3, :], 1.0, 0.0)
-    for c in range(3):
-        left = jnp.where(hit, amps_v[c : c + 1, :], 0.0)
-        source[c] = lax.dot_general(
-            left, hit_z, (((1,), (1,)), ((), ())),
-            precision=lax.Precision.HIGHEST, preferred_element_type=jnp.float32,
-        ).reshape(YY, SUB, LANES)
 
     shape = (BX, LANES)
     r = iota(shape, 0)
@@ -191,13 +133,124 @@
             for n in (0, 1):
                 gain[n, c, :, lanes] = design * gains[n]
 
-    remote(part(core), body.at[other, span(core)], (0, 0), (gx, gy, other)).wait_recv()
-    for h in (0, 1):
-        remote(packed.at[0], body.at[h, 5 * core], (0, 1 + h), (gx, gy, other)).wait_recv()
+    lane_g = iota((BX, LANES), 1)
+    firsts, lasts = [], []
+    for n, c in ((0, 0), (0, 2), (1, 1)):
+        one, two = gain[n, c], gain[n + (c == 2), (c + 1) % 3]
+        firsts.append(jnp.where(lane_g < 64, one[:, :LANES], roll(two[:, :LANES], 64, 1)))
+        lasts.append(jnp.where(lane_g < 64, roll(two[:, LANES:], 64, 1), one[:, LANES:]))
+    none2, none4 = jnp.zeros((2, LANES), jnp.float32), jnp.zeros((4, 2 * LANES), jnp.float32)
+    for side, x in ((0, 0), (1, BX - 2)):
+        sx[side] = jnp.concatenate([gain[n, c, x : x + 2, :] for n in (0, 1) for c in range(3)] + [none4], axis=0)
+        for k, tiles in ((0, firsts), (1, lasts)):
+            sc[side, k] = jnp.concatenate([t[x : x + 2] for t in tiles] + [none2], axis=0)
+    for m in range(3):
+        sy[0, m], sy[1, m] = firsts[m], lasts[m]
+
+    def remote(src, dst, role, device):
+        return pltpu.make_async_remote_copy(
+            src_ref=src,
+            dst_ref=dst,
+            send_sem=send_sem.at[role[0]],
+            recv_sem=recv_sem.at[role[1]],
+            device_id=device,
+            device_id_type=pl.DeviceIdType.MESH,
+        )
+
+    def sends_of(half):
+        if half == 0:
+            last, first, low, high = pl.ds(6, 2), pl.ds(0, 2), pl.ds(0, 6), pl.ds(2, 6)
+            body, halo, at_low, at_high = body0, halo0, pl.ds(0, 2), pl.ds(6, 2)
+            to_low, to_high = pl.ds(2, 6), pl.ds(0, 6)
+            rows, places = (pl.ds(0, 32), pl.ds(0, 32)), (pl.ds(0, 32), pl.ds(32, 32))
+        else:
+            last, first, low, high = pl.ds(7, 1), pl.ds(0, 1), pl.ds(0, 5), pl.ds(3, 5)
+            body, halo, at_low, at_high = body1, halo1, pl.ds(0, 1), pl.ds(5, 1)
+            to_low, to_high = pl.ds(1, 5), pl.ds(0, 5)
+            rows, places = (pl.ds(0, 16), pl.ds(16, 16)), (pl.ds(0, 16), pl.ds(48, 16))
+        sides = ((0, down_x), (1, up_x))
+        sends = []
+        for side, to_x in sides:
+            row, place = rows[side], places[side]
+            role = 7 + 2 * side + half
+            sends += [
+                remote(edge.at[side, last, row], halo.at[at_low, place], (3 + 4 * side, role), (to_x, up_y, 0)),
+                remote(edge.at[side, first, row], halo.at[at_high, place], (4 + 4 * side, role), (to_x, down_y, 1)),
+            ]
+        sends += [
+            remote(packed.at[last], body.at[at_low], (1, 1 + half), (gx, up_y, 0)),
+            remote(packed.at[first], body.at[at_high], (2, 1 + half), (gx, down_y, 1)),
+        ]
+        for side, to_x in sides:
+            row, place = rows[side], places[side]
+            role = 3 + 2 * side + half
+            sends += [
+                remote(edge.at[side, low, row], halo.at[to_low, place], (5 + 4 * side, role), (to_x, gy, 0)),
+                remote(edge.at[side, high, row], halo.at[to_high, place], (6 + 4 * side, role), (to_x, gy, 1)),
+            ]
+        part, span = (high, to_high) if half == 0 else (low, to_low)
+        sends.append(remote(packed.at[part], body.at[span], (0, 0), (gx, gy, 1 - half)))
+        return sends
+
+    above = (gx, jnp.where(core == 0, gy, up_y), other)
+    below = (gx, jnp.where(core == 0, down_y, gy), other)
+    swaps = [
+        remote(sc.at[0, 0], g_c.at[0, 0], (14, 14), (down_x,) + below[1:]),
+        remote(sc.at[0, 1], g_c.at[0, 1], (15, 15), (down_x,) + above[1:]),
+        remote(sc.at[1, 0], g_c.at[1, 0], (16, 16), (up_x,) + below[1:]),
+        remote(sc.at[1, 1], g_c.at[1, 1], (17, 17), (up_x,) + above[1:]),
+        remote(sy.at[0], g_y.at[0], (12, 12), below),
+        remote(sy.at[1], g_y.at[1], (13, 13), above),
+        remote(sx.at[0], g_x.at[0], (18, 18), (down_x, gy, core)),
+        remote(sx.at[1], g_x.at[1], (19, 19), (up_x, gy, core)),
+    ]
+
+    pl.semaphore_wait(barrier, len(senders))
+    for half in (0, 1):
+        @pl.when(core == half)
+        def _(half=half):
+            for send in sends_of(half):
+                send.start()
+            if half == 0:
+                body0[2:8] = packed[0:6]
+            else:
+                body1[0:5] = packed[3:8]
+    for swap in swaps:
+        swap.start()
+
+    y_first = gy * BY + core * HY - WIDE
+    row = iota((YY * SUB, 64), 0)
+    sub = row & (SUB - 1)
+    row_x = gx * BX + jnp.where(sub < 12, sub, sub - SUB)
+    row_y = y_first + (row >> 4)
+    hit = (row_x == cells_v[0:1, :]) & (row_y == cells_v[1:2, :])
+    hit_z = jnp.where(iota((LANES, 64), 0) == cells_v[2:3, :], 1.0, 0.0)
+    for c in range(3):
+        left = jnp.where(hit, amps_v[c : c + 1, :], 0.0)
+        source[c] = lax.dot_general(
+            left, hit_z, (((1,), (1,)), ((), ())),
+            precision=lax.Precision.HIGHEST, preferred_element_type=jnp.float32,
+        ).reshape(YY, SUB, LANES)
+
+    here = (gx, gy, other)
+    for half in (0, 1):
+        @pl.when(core != half)
+        def _(half=half):
+            if half == 0:
+                remote(packed.at[pl.ds(2, 6)], body0.at[pl.ds(0, 6)], (0, 0), here).wait_recv()
+            else:
+                remote(packed.at[pl.ds(0, 5)], body1.at[pl.ds(1, 5)], (0, 0), here).wait_recv()
+
+        body, halo = (body0, halo0) if half == 0 else (body1, halo1)
+        face, long, rows = (2, 6, 32) if half == 0 else (1, 5, 16)
+        at_face = pl.ds(6 * core if half == 0 else 5 * core, face)
+        span = pl.ds(2 - 2 * core if half == 0 else 1 - core, long)
+        remote(packed.at[pl.ds(0, face)], body.at[at_face], (0, 1 + half), here).wait_recv()
         for side in (0, 1):
-            place = pl.ds(48 * side, 16)
-            remote(edge.at[0, pl.ds(0, SENT)], halo.at[h, span(core), place], (0, 3 + 2 * side + h), (gx, gy, other)).wait_recv()
-            remote(edge.at[0, 0], halo.at[h, 5 * core, place], (0, 7 + 2 * side + h), (gx, gy, other)).wait_recv()
+            place = pl.ds((64 - rows) * side, rows)
+            x_part, corner = edge.at[0, pl.ds(0, long), pl.ds(0, rows)], edge.at[0, pl.ds(0, face), pl.ds(0, rows)]
+            remote(x_part, halo.at[span, place], (0, 3 + 2 * side + half), here).wait_recv()
+            remote(corner, halo.at[at_face, place], (0, 7 + 2 * side + half), here).wait_recv()
 
     x_of = iota((SUB, LANES), 0)
     x_of = gx * BX + jnp.where(x_of < 12, x_of, x_of - SUB)
@@ -214,8 +267,12 @@
         return even, odd
 
     for pair in range(YY // 2):
-        own = merge(body[0, pair], body[1, pair], lane_b)
-        beside = merge(halo[0, pair], halo[1, pair], lane_h)
+        if 1 <= pair <= PAIRS - 2:
+            upper_own, upper_beside = body1[pair - 1], halo1[pair - 1]
+        else:
+            upper_own, upper_beside = jnp.zeros((ROWS, LANES), jnp.float32), jnp.zeros((64, LANES), jnp.float32)
+        own = merge(body0[pair], upper_own, lane_b)
+        beside = merge(halo0[pair], upper_beside, lane_h)
         for k in (0, 1):
             merged[k] = beside[k]
             yy = 2 * pair + k
@@ -258,61 +315,33 @@
 
         lax.fori_loop(first, last, step, 0, unroll=True)
 
-    quarter = iota((BX, LANES), 1) >> 5
+    quarter = iota((SUB, LANES), 1) >> 5
 
     def flatten(time):
         for c in range(3):
-            for tile in (0, 1):
-                out = jnp.zeros((BX, LANES), jnp.float32)
-                for q in range(4):
-                    v = fields[c, 2 + 4 * tile + q, 0:BX, :]
+            for tile, first, quarters in ((0, 0, range(4)), (1, 4, range(4)), (2, 8, (0, 1)), (3, -4, (2, 3))):
+                out = jnp.zeros((SUB, LANES), jnp.float32)
+                for q in quarters:
+                    v = fields[c, WIDE + first + q]
                     out = jnp.where(quarter == q, roll(v, SLAB * q - BOTTOM, 1), out)
                 flat[time, c, :, pl.ds(LANES * tile, LANES)] = out
 
-    magnetic_rows(0, 11)
-    electric_rows(1, 11, 0)
+    magnetic_rows(0, YY - 1)
+    electric_rows(1, YY - 1, 0)
     flatten(0)
-    magnetic_rows(1, 10)
-    electric_rows(2, 10, 1)
-    flatten(1)
-
-    shape = (BX, 2 * LANES)
-    total = jnp.zeros(shape, jnp.float32)
-    for n in (0, 1):
-        for c in range(3):
-            total = total + gain[n, c] * flat[n, c]
-
-    z = iota(shape, 1) & (SLAB - 1)
-    folded = total
-    for by in (-2, -1, 1, 2):
-        ok = same_pixel(z, anchor[2], by) & (z + by >= 0) & (z + by < SLAB)
-        folded = folded + jnp.where(ok, roll(total, -by, 1), 0.0)
-    g_send[...] = folded
-
-    above = (gx, jnp.where(core == 0, gy, up_y), other)
-    below = (gx, jnp.where(core == 0, down_y, gy), other)
-    first_rows, last_rows = g_send.at[:, pl.ds(0, LANES)], g_send.at[:, pl.ds(LANES, LANES)]
-    swaps = [
-        remote(first_rows, g_y.at[0], (12, 12), below),
-        remote(last_rows, g_y.at[1], (13, 13), above),
-        remote(first_rows, g_c.at[0, 0], (14, 14), (down_x,) + below[1:]),
-        remote(last_rows, g_c.at[0, 1], (15, 15), (down_x,) + above[1:]),
-        remote(first_rows, g_c.at[1, 0], (16, 16), (up_x,) + below[1:]),
-        remote(last_rows, g_c.at[1, 1], (17, 17), (up_x,) + above[1:]),
-        remote(g_send, g_x.at[0], (18, 18), (down_x, gy, core)),
-        remote(g_send, g_x.at[1], (19, 19), (up_x, gy, core)),
-    ]
-    for swap in swaps:
-        swap.start()
+    magnetic_rows(1, YY - 2)
+    electric_rows(2, YY - 2, 1)
 
     for y in range(HY):
-        v = jnp.concatenate([fields[c, 2 + y, 0:BX, :] for c in range(3)], axis=0)
+        v = jnp.concatenate([fields[c, WIDE + y, 0:BX, :] for c in range(3)], axis=0)
         moved = roll(v, -CZ, 1)
         first = core == 0
         fe[pl.ds(HY * core + y, 3 * BX, stride=BY), :] = jnp.where(first, v, moved)[:, :CZ]
         fe_send[y] = jnp.where(first, moved, v)
     fe_copy = remote(fe_send, fe_recv, (11, 11), (gx, gy, other))
     fe_copy.start()
+
+    flatten(1)
 
     for t in (0, 1):
         lanes = pl.ds(LANES * t, LANES)
@@ -321,8 +350,8 @@
                 for c in range(3):
                     rows = pl.ds(3 * FREQ * p + 3 * f + c, BX, stride=6 * FREQ)
                     adj_v[t, rows, :] = (
-                        weights[f : f + 1, :] * flat[0, c, :, lanes]
-                        + weights[FREQ + f : FREQ + f + 1, :] * flat[1, c, :, lanes]
+                        weights[f : f + 1, :] * flat[0, c, 0:BX, lanes]
+                        + weights[FREQ + f : FREQ + f + 1, :] * flat[1, c, 0:BX, lanes]
                     )
     stores = [
         pltpu.make_async_copy(adj_v.at[t], adj.at[:, pl.ds(LANES * t, LANES)], load_sem.at[11 + t]) for t in (0, 1)
@@ -330,29 +359,43 @@
     for store in stores:
         store.start()
 
-    fe_copy.wait_recv()
-    for y in range(HY):
-        fe[pl.ds(HY * other + y, 3 * BX, stride=BY), :] = fe_recv[y][:, :CZ]
-
     for swap in swaps:
         swap.wait_recv()
     block = gy * 2 + core
-    wide = (BX, 4 * LANES)
-    tile0 = jnp.concatenate([folded, g_y[0], g_y[1]], axis=1)
-    upper = jnp.concatenate([g_x[0], g_c[0, 0], g_c[0, 1]], axis=1)
-    lower = jnp.concatenate([g_x[1], g_c[1, 0], g_c[1, 1]], axis=1)
-    x_row, column = iota(wide, 0), iota(wide, 1)
-    upper = jnp.where(gx < nx - 1, upper, 0.0)
-    lower = jnp.where(gx > 0, lower, 0.0)
-    tile1 = jnp.where(x_row < 4, upper, lower)
-    y_ok = (column < 2 * LANES) | ((column < 3 * LANES) & (block < 2 * ny - 1)) | ((column >= 3 * LANES) & (block > 0))
-    extended = jnp.where(
-        jnp.concatenate([y_ok, y_ok], axis=0), jnp.concatenate([tile0, tile1], axis=0), 0.0
-    )
+    wide = (SUB, 4 * LANES)
+    total = jnp.zeros(wide, jnp.float32)
+    gap2 = jnp.zeros((4, 2 * LANES), jnp.float32)
+    gap1 = jnp.zeros((4, LANES), jnp.float32)
+    for n in (0, 1):
+        for c in range(3):
+            k = 3 * n + c
+            two = pl.ds(2 * k, 2)
+            pair = pl.ds(2 * (k // 2), 2)
+            tile1 = jnp.concatenate([g_x[0, two, :], gap2, g_x[1, two, :]], axis=0)
+            beyond = []
+            for up in (0, 1):
+                corner = jnp.concatenate([g_c[0, up, pair, :], gap1, g_c[1, up, pair, :]], axis=0)
+                both = jnp.concatenate([g_y[up, k // 2], corner], axis=0)
+                beyond.append(roll(both, 64, 1) if k % 2 else both)
+            weight = jnp.concatenate([jnp.concatenate([gain[n, c], tile1], axis=0)] + beyond, axis=1)
+            total = total + weight * flat[n, c]
+    row, column = iota(wide, 0), iota(wide, 1)
+    x_all = gx * BX + jnp.where(row < 12, row, row - SUB)
+    here_ok = (x_all >= 0) & (x_all < nx * BX)
+    here_ok = here_ok & ((column < 3 * LANES) | (block > 0)) & ((column < 2 * LANES) | (column >= 3 * LANES) | (block < 2 * ny - 1))
+    total = jnp.where(here_ok, total, 0.0)
+
+    z = column & (SLAB - 1)
+    extended = total
+    for by in (-2, -1, 1, 2):
+        ok = same_pixel(z, anchor[2], by) & (z + by >= 0) & (z + by < SLAB)
+        extended = extended + jnp.where(ok, roll(total, -by, 1), 0.0)
+    x_row = gx * BX + iota((BX, 4 * LANES), 0)
     along_x = extended[:BX]
     for by in (-2, -1, 1, 2):
-        ok = same_pixel(gx * BX + x_row, anchor[0], by)
+        ok = same_pixel(x_row, anchor[0], by)
         along_x = along_x + jnp.where(ok, roll(extended, -by, 0)[:BX], 0.0)
+    shape = (BX, 2 * LANES)
     result = along_x[:, : 2 * LANES]
     y_row = block * HY + (iota(shape, 1) >> 5)
     for by in (-2, -1, 1, 2):
@@ -360,7 +403,16 @@
         result = result + jnp.where(ok, roll(along_x, -SLAB * by, 1)[:, : 2 * LANES], 0.0)
     grad[...] = result
 
-    for send in sends + [fe_copy] + swaps:
+    fe_copy.wait_recv()
+    for y in range(HY):
+        fe[pl.ds(HY * other + y, 3 * BX, stride=BY), :] = fe_recv[y][:, :CZ]
+
+    for half in (0, 1):
+        @pl.when(core == half)
+        def _(half=half):
+            for send in sends_of(half):
+                send.wait_send()
+    for send in [fe_copy] + swaps:
         send.wait_send()
     for store in stores:
         store.wait()
@@ -406,19 +458,23 @@
             pltpu.VMEM((2, BX * 6 * FREQ, LANES), f32),
             pltpu.VMEM((BX * BY, CZ), f32),
             pltpu.VMEM((PAIRS, ROWS, LANES), f32),
-            pltpu.VMEM((2, PAIRS, 16, LANES), f32),
-            pltpu.VMEM((2, YY // 2, ROWS, LANES), f32),
-            pltpu.VMEM((2, YY // 2, 64, LANES), f32),
+            pltpu.VMEM((2, PAIRS, 8 * WIDE, LANES), f32),
+            pltpu.VMEM((PAIRS, ROWS, LANES), f32),
+            pltpu.VMEM((PAIRS - 2, ROWS, LANES), f32),
+            pltpu.VMEM((PAIRS, 64, LANES), f32),
+            pltpu.VMEM((PAIRS - 2, 64, LANES), f32),
             pltpu.VMEM((2, 64, LANES), f32),
             pltpu.VMEM((COMPS, YY, SUB, LANES), f32),
             pltpu.VMEM((3, YY, SUB, LANES), f32),
             pltpu.VMEM((2, 3, BX, 2 * LANES), f32),
-            pltpu.VMEM((2, 3, BX, 2 * LANES), f32),
+            pltpu.VMEM((2, 3, SUB, 4 * LANES), f32),
             pltpu.VMEM((HY, 3 * BX, LANES), f32),
             pltpu.VMEM((HY, 3 * BX, LANES), f32),
-            pltpu.VMEM((BX, 2 * LANES), f32),
-            pltpu.VMEM((2, BX, 2 * LANES), f32),
-            pltpu.VMEM((2, BX, LANES), f32),
+            pltpu.VMEM((2, 16, 2 * LANES), f32),
+            pltpu.VMEM((2, 3, BX, LANES), f32),
+            pltpu.VMEM((2, 2, BX, LANES), f32),
+            pltpu.VMEM((2, 16, 2 * LANES), f32),
+            pltpu.VMEM((2, 3, BX, LANES), f32),
             pltpu.VMEM((2, 2, BX, LANES), f32),
             pltpu.SemaphoreType.DMA((13,)),
             pltpu.SemaphoreType.DMA((20,)),

time: 39 us -> 40.7 us (1.044); the launches traced: 38.4 us -> 40.5 us
  Pallas kernels: 37.7 us -> 39.9 us
    pallas_call x1, Pallas kernels: 37 us -> 39.1 us  [body_fn(): pl.pallas_call(kernel, out_shape=(jax.ShapeDtypeStruct((BX * 6 * FREQ, 2...]
where the time goes in v3:
time: 40.7 us; the launch traced here: 40.5 us
  Pallas kernels  39.9 us (98%)
  between operations  0.64 us (2%)
    pallas_call x1, Pallas kernels, body_fn(): pl.pallas_call(kernel, out_shape=(jax.ShapeDtypeStruct((BX * 6 * FREQ, 2...  39.1 us

profile of v3, /device:TPU:1, one launch (start us, length us, event | category | flops | bytes accessed | tf_op | source)
XLA Modules:
  0.0 40.5 jit_solution(9762288198941669489)
XLA Ops:
  0.6 39.1 %shard_map.121 = (f32[192,256]{1,0:T(8,128)S(1)}, f32[8,256]{1,0:T(8,128)S(1)}, f32[384,48]{1,0:T(8,128)S(1)}) custom-call(f32[384,48]{1,0:T(8,128)} %bitcast.8, f32[384,48]{1,0:T(8,128)} %bitcast.9, s32[128,48]{1,0:T(8,128)} %bitcast.11, f32[4]{0:T(128)} %perm_in.1, s32[3,64]{1,0:T(4,128)} %bitcast.12, f32[3,64]{1,0:T(4,128)} %bitcast.13, f32[4]{0:T(128)} %omegas_in.1, ...), custom_call_target="tpu_custom_call" | custom-call | tf_op jit(solution)/shard_map/pallas_call | solution.py:438
  39.8 0.8 %shard_map.122 = (f32[192,256]{1,0:T(8,128)}, f32[8,256]{1,0:T(8,128)}, f32[384,48]{1,0:T(8,128)}) custom-call(f32[192,256]{1,0:T(8,128)S(1)} %get-tuple-element.9.adj, f32[8,256]{1,0:T(8,128)S(1)} %get-tuple-element.10.grad, f32[384,48]{1,0:T(8,128)S(1)} %get-tuple-element.11.fe), custom_call_target="tpu_custom_call" | custom-call | tf_op jit(solution)/shard_map/pallas_call | solution.py:503

commit v4 on v3

--- a/solution.py
+++ b/solution.py
@@ -22,7 +22,7 @@
 PAIRS = BY // 2
 WIDE = 4
 YY = HY + 2 * WIDE
-SUB = BX + 2 * WIDE
+SUB = 16
 
 
 def roll(v, by, axis):
@@ -49,7 +49,7 @@
     perm, omegas, anchor,
     e_v, h_v, mat_v, cells_v, amps_v, mask_v, fwd_v, adj_v, coef_v,
     packed, edge, body0, body1, halo0, halo1, merged, fields, source, gain, flat,
-    fe_send, fe_recv, sx, sy, sc, g_x, g_y, g_c,
+    fe_send, fe_recv, sy, g_y, g_send, g_x,
     load_sem, send_sem, recv_sem,
 ):
     nx, ny = lax.axis_size("gx"), lax.axis_size("gy")
@@ -60,10 +60,8 @@
 
     barrier = pltpu.get_barrier_semaphore()
     face_y = jnp.where(core == 0, down_y, up_y)
-    senders = [(gx, gy, other)]
-    for h in (0, 1):
-        senders += [(up_x, gy, h), (down_x, gy, h)]
-        senders += [(gx, face_y, h), (up_x, face_y, h), (down_x, face_y, h)]
+    senders = [(x, face_y, h) for x in (up_x, down_x, gx) for h in (0, 1)]
+    senders += [(x, gy, h) for x in (up_x, down_x) for h in (0, 1)] + [(gx, gy, other)]
     for sender in senders:
         pl.semaphore_signal(barrier, inc=1, device_id=sender, device_id_type=pl.DeviceIdType.MESH)
 
@@ -79,6 +77,7 @@
         load.start()
 
     edge[...] = jnp.zeros_like(edge)
+    halo0[:, 16:48, :] = jnp.zeros((PAIRS, 32, LANES), jnp.float32)
     halo1[:, 16:48, :] = jnp.zeros((PAIRS - 2, 32, LANES), jnp.float32)
 
     for load in loads[:4]:
@@ -104,8 +103,10 @@
         packed[pair] = jnp.concatenate(rows + [blank], axis=1)
     for pair in range(PAIRS):
         for side in (0, 1):
-            for x in range(WIDE):
-                edge[side, pair, pl.ds(8 * x, COMPS), :] = packed[pair, pl.ds(WIDE * side + x, COMPS, stride=BX), :]
+            for x in (0, 1):
+                edge[side, pair, pl.ds(8 * x, COMPS), :] = packed[
+                    pair, pl.ds((BX - 2) * side + x, COMPS, stride=BX), :
+                ]
     for load in loads[4:]:
         load.wait()
 
@@ -139,11 +140,6 @@
         one, two = gain[n, c], gain[n + (c == 2), (c + 1) % 3]
         firsts.append(jnp.where(lane_g < 64, one[:, :LANES], roll(two[:, :LANES], 64, 1)))
         lasts.append(jnp.where(lane_g < 64, roll(two[:, LANES:], 64, 1), one[:, LANES:]))
-    none2, none4 = jnp.zeros((2, LANES), jnp.float32), jnp.zeros((4, 2 * LANES), jnp.float32)
-    for side, x in ((0, 0), (1, BX - 2)):
-        sx[side] = jnp.concatenate([gain[n, c, x : x + 2, :] for n in (0, 1) for c in range(3)] + [none4], axis=0)
-        for k, tiles in ((0, firsts), (1, lasts)):
-            sc[side, k] = jnp.concatenate([t[x : x + 2] for t in tiles] + [none2], axis=0)
     for m in range(3):
         sy[0, m], sy[1, m] = firsts[m], lasts[m]
 
@@ -162,31 +158,29 @@
             last, first, low, high = pl.ds(6, 2), pl.ds(0, 2), pl.ds(0, 6), pl.ds(2, 6)
             body, halo, at_low, at_high = body0, halo0, pl.ds(0, 2), pl.ds(6, 2)
             to_low, to_high = pl.ds(2, 6), pl.ds(0, 6)
-            rows, places = (pl.ds(0, 32), pl.ds(0, 32)), (pl.ds(0, 32), pl.ds(32, 32))
         else:
             last, first, low, high = pl.ds(7, 1), pl.ds(0, 1), pl.ds(0, 5), pl.ds(3, 5)
             body, halo, at_low, at_high = body1, halo1, pl.ds(0, 1), pl.ds(5, 1)
             to_low, to_high = pl.ds(1, 5), pl.ds(0, 5)
-            rows, places = (pl.ds(0, 16), pl.ds(16, 16)), (pl.ds(0, 16), pl.ds(48, 16))
         sides = ((0, down_x), (1, up_x))
         sends = []
         for side, to_x in sides:
-            row, place = rows[side], places[side]
+            place = pl.ds(48 * side, 16)
             role = 7 + 2 * side + half
             sends += [
-                remote(edge.at[side, last, row], halo.at[at_low, place], (3 + 4 * side, role), (to_x, up_y, 0)),
-                remote(edge.at[side, first, row], halo.at[at_high, place], (4 + 4 * side, role), (to_x, down_y, 1)),
+                remote(edge.at[side, last], halo.at[at_low, place], (3 + 4 * side, role), (to_x, up_y, 0)),
+                remote(edge.at[side, first], halo.at[at_high, place], (4 + 4 * side, role), (to_x, down_y, 1)),
             ]
         sends += [
             remote(packed.at[last], body.at[at_low], (1, 1 + half), (gx, up_y, 0)),
             remote(packed.at[first], body.at[at_high], (2, 1 + half), (gx, down_y, 1)),
         ]
         for side, to_x in sides:
-            row, place = rows[side], places[side]
+            place = pl.ds(48 * side, 16)
             role = 3 + 2 * side + half
             sends += [
-                remote(edge.at[side, low, row], halo.at[to_low, place], (5 + 4 * side, role), (to_x, gy, 0)),
-                remote(edge.at[side, high, row], halo.at[to_high, place], (6 + 4 * side, role), (to_x, gy, 1)),
+                remote(edge.at[side, low], halo.at[to_low, place], (5 + 4 * side, role), (to_x, gy, 0)),
+                remote(edge.at[side, high], halo.at[to_high, place], (6 + 4 * side, role), (to_x, gy, 1)),
             ]
         part, span = (high, to_high) if half == 0 else (low, to_low)
         sends.append(remote(packed.at[part], body.at[span], (0, 0), (gx, gy, 1 - half)))
@@ -194,16 +188,7 @@
 
     above = (gx, jnp.where(core == 0, gy, up_y), other)
     below = (gx, jnp.where(core == 0, down_y, gy), other)
-    swaps = [
-        remote(sc.at[0, 0], g_c.at[0, 0], (14, 14), (down_x,) + below[1:]),
-        remote(sc.at[0, 1], g_c.at[0, 1], (15, 15), (down_x,) + above[1:]),
-        remote(sc.at[1, 0], g_c.at[1, 0], (16, 16), (up_x,) + below[1:]),
-        remote(sc.at[1, 1], g_c.at[1, 1], (17, 17), (up_x,) + above[1:]),
-        remote(sy.at[0], g_y.at[0], (12, 12), below),
-        remote(sy.at[1], g_y.at[1], (13, 13), above),
-        remote(sx.at[0], g_x.at[0], (18, 18), (down_x, gy, core)),
-        remote(sx.at[1], g_x.at[1], (19, 19), (up_x, gy, core)),
-    ]
+    beside = [remote(sy.at[0], g_y.at[0], (12, 12), below), remote(sy.at[1], g_y.at[1], (13, 13), above)]
 
     pl.semaphore_wait(barrier, len(senders))
     for half in (0, 1):
@@ -215,8 +200,8 @@
                 body0[2:8] = packed[0:6]
             else:
                 body1[0:5] = packed[3:8]
-    for swap in swaps:
-        swap.start()
+    for send in beside:
+        send.start()
 
     y_first = gy * BY + core * HY - WIDE
     row = iota((YY * SUB, 64), 0)
@@ -242,13 +227,13 @@
                 remote(packed.at[pl.ds(0, 5)], body1.at[pl.ds(1, 5)], (0, 0), here).wait_recv()
 
         body, halo = (body0, halo0) if half == 0 else (body1, halo1)
-        face, long, rows = (2, 6, 32) if half == 0 else (1, 5, 16)
+        face, long = (2, 6) if half == 0 else (1, 5)
         at_face = pl.ds(6 * core if half == 0 else 5 * core, face)
         span = pl.ds(2 - 2 * core if half == 0 else 1 - core, long)
         remote(packed.at[pl.ds(0, face)], body.at[at_face], (0, 1 + half), here).wait_recv()
         for side in (0, 1):
-            place = pl.ds((64 - rows) * side, rows)
-            x_part, corner = edge.at[0, pl.ds(0, long), pl.ds(0, rows)], edge.at[0, pl.ds(0, face), pl.ds(0, rows)]
+            place = pl.ds(48 * side, 16)
+            x_part, corner = edge.at[0, pl.ds(0, long)], edge.at[0, pl.ds(0, face)]
             remote(x_part, halo.at[span, place], (0, 3 + 2 * side + half), here).wait_recv()
             remote(corner, halo.at[at_face, place], (0, 7 + 2 * side + half), here).wait_recv()
 
@@ -272,9 +257,9 @@
         else:
             upper_own, upper_beside = jnp.zeros((ROWS, LANES), jnp.float32), jnp.zeros((64, LANES), jnp.float32)
         own = merge(body0[pair], upper_own, lane_b)
-        beside = merge(halo0[pair], upper_beside, lane_h)
+        edges = merge(halo0[pair], upper_beside, lane_h)
         for k in (0, 1):
-            merged[k] = beside[k]
+            merged[k] = edges[k]
             yy = 2 * pair + k
             y = y_first + yy
             ok = inside & (y >= 0) & (y < y_end)
@@ -315,14 +300,14 @@
 
         lax.fori_loop(first, last, step, 0, unroll=True)
 
-    quarter = iota((SUB, LANES), 1) >> 5
+    quarter = iota((BX, LANES), 1) >> 5
 
     def flatten(time):
         for c in range(3):
             for tile, first, quarters in ((0, 0, range(4)), (1, 4, range(4)), (2, 8, (0, 1)), (3, -4, (2, 3))):
-                out = jnp.zeros((SUB, LANES), jnp.float32)
+                out = jnp.zeros((BX, LANES), jnp.float32)
                 for q in quarters:
-                    v = fields[c, WIDE + first + q]
+                    v = fields[c, WIDE + first + q, 0:BX, :]
                     out = jnp.where(quarter == q, roll(v, SLAB * q - BOTTOM, 1), out)
                 flat[time, c, :, pl.ds(LANES * tile, LANES)] = out
 
@@ -331,6 +316,40 @@
     flatten(0)
     magnetic_rows(1, YY - 2)
     electric_rows(2, YY - 2, 1)
+
+    flatten(1)
+    for send in beside:
+        send.wait_recv()
+    block = gy * 2 + core
+    wide = (BX, 4 * LANES)
+    total = jnp.zeros(wide, jnp.float32)
+    for n in (0, 1):
+        for c in range(3):
+            k = 3 * n + c
+            beyond = [roll(g_y[up, k // 2], 64, 1) if k % 2 else g_y[up, k // 2] for up in (0, 1)]
+            total = total + jnp.concatenate([gain[n, c]] + beyond, axis=1) * flat[n, c]
+    column = iota(wide, 1)
+    y_ok = ((column < 3 * LANES) | (block > 0)) & ((column < 2 * LANES) | (column >= 3 * LANES) | (block < 2 * ny - 1))
+    total = jnp.where(y_ok, total, 0.0)
+
+    z = column & (SLAB - 1)
+    along_z = total
+    for by in (-2, -1, 1, 2):
+        ok = same_pixel(z, anchor[2], by) & (z + by >= 0) & (z + by < SLAB)
+        along_z = along_z + jnp.where(ok, roll(total, -by, 1), 0.0)
+    shape = (BX, 2 * LANES)
+    folded = along_z[:, : 2 * LANES]
+    y_row = block * HY + (iota(shape, 1) >> 5)
+    for by in (-2, -1, 1, 2):
+        ok = same_pixel(y_row, anchor[1], by)
+        folded = folded + jnp.where(ok, roll(along_z, -SLAB * by, 1)[:, : 2 * LANES], 0.0)
+    g_send[...] = folded
+    swaps = [
+        remote(g_send, g_x.at[0], (14, 14), (down_x, gy, core)),
+        remote(g_send, g_x.at[1], (15, 15), (up_x, gy, core)),
+    ]
+    for swap in swaps:
+        swap.start()
 
     for y in range(HY):
         v = jnp.concatenate([fields[c, WIDE + y, 0:BX, :] for c in range(3)], axis=0)
@@ -341,8 +360,6 @@
     fe_copy = remote(fe_send, fe_recv, (11, 11), (gx, gy, other))
     fe_copy.start()
 
-    flatten(1)
-
     for t in (0, 1):
         lanes = pl.ds(LANES * t, LANES)
         for f in range(FREQ):
@@ -350,8 +367,8 @@
                 for c in range(3):
                     rows = pl.ds(3 * FREQ * p + 3 * f + c, BX, stride=6 * FREQ)
                     adj_v[t, rows, :] = (
-                        weights[f : f + 1, :] * flat[0, c, 0:BX, lanes]
-                        + weights[FREQ + f : FREQ + f + 1, :] * flat[1, c, 0:BX, lanes]
+                        weights[f : f + 1, :] * flat[0, c, :, lanes]
+                        + weights[FREQ + f : FREQ + f + 1, :] * flat[1, c, :, lanes]
                     )
     stores = [
         pltpu.make_async_copy(adj_v.at[t], adj.at[:, pl.ds(LANES * t, LANES)], load_sem.at[11 + t]) for t in (0, 1)
@@ -359,60 +376,28 @@
     for store in stores:
         store.start()
 
-    for swap in swaps:
-        swap.wait_recv()
-    block = gy * 2 + core
-    wide = (SUB, 4 * LANES)
-    total = jnp.zeros(wide, jnp.float32)
-    gap2 = jnp.zeros((4, 2 * LANES), jnp.float32)
-    gap1 = jnp.zeros((4, LANES), jnp.float32)
-    for n in (0, 1):
-        for c in range(3):
-            k = 3 * n + c
-            two = pl.ds(2 * k, 2)
-            pair = pl.ds(2 * (k // 2), 2)
-            tile1 = jnp.concatenate([g_x[0, two, :], gap2, g_x[1, two, :]], axis=0)
-            beyond = []
-            for up in (0, 1):
-                corner = jnp.concatenate([g_c[0, up, pair, :], gap1, g_c[1, up, pair, :]], axis=0)
-                both = jnp.concatenate([g_y[up, k // 2], corner], axis=0)
-                beyond.append(roll(both, 64, 1) if k % 2 else both)
-            weight = jnp.concatenate([jnp.concatenate([gain[n, c], tile1], axis=0)] + beyond, axis=1)
-            total = total + weight * flat[n, c]
-    row, column = iota(wide, 0), iota(wide, 1)
-    x_all = gx * BX + jnp.where(row < 12, row, row - SUB)
-    here_ok = (x_all >= 0) & (x_all < nx * BX)
-    here_ok = here_ok & ((column < 3 * LANES) | (block > 0)) & ((column < 2 * LANES) | (column >= 3 * LANES) | (block < 2 * ny - 1))
-    total = jnp.where(here_ok, total, 0.0)
-
-    z = column & (SLAB - 1)
-    extended = total
-    for by in (-2, -1, 1, 2):
-        ok = same_pixel(z, anchor[2], by) & (z + by >= 0) & (z + by < SLAB)
-        extended = extended + jnp.where(ok, roll(total, -by, 1), 0.0)
-    x_row = gx * BX + iota((BX, 4 * LANES), 0)
-    along_x = extended[:BX]
-    for by in (-2, -1, 1, 2):
-        ok = same_pixel(x_row, anchor[0], by)
-        along_x = along_x + jnp.where(ok, roll(extended, -by, 0)[:BX], 0.0)
-    shape = (BX, 2 * LANES)
-    result = along_x[:, : 2 * LANES]
-    y_row = block * HY + (iota(shape, 1) >> 5)
-    for by in (-2, -1, 1, 2):
-        ok = same_pixel(y_row, anchor[1], by)
-        result = result + jnp.where(ok, roll(along_x, -SLAB * by, 1)[:, : 2 * LANES], 0.0)
-    grad[...] = result
-
     fe_copy.wait_recv()
     for y in range(HY):
         fe[pl.ds(HY * other + y, 3 * BX, stride=BY), :] = fe_recv[y][:, :CZ]
+
+    for swap in swaps:
+        swap.wait_recv()
+    x_row = iota(shape, 0)
+    upper = jnp.where(gx < nx - 1, g_x[0], 0.0)
+    lower = jnp.where(gx > 0, g_x[1], 0.0)
+    extended = jnp.concatenate([folded, jnp.where(x_row < 4, upper, lower)], axis=0)
+    result = folded
+    for by in (-2, -1, 1, 2):
+        ok = same_pixel(gx * BX + x_row, anchor[0], by)
+        result = result + jnp.where(ok, roll(extended, -by, 0)[:BX], 0.0)
+    grad[...] = result
 
     for half in (0, 1):
         @pl.when(core == half)
         def _(half=half):
             for send in sends_of(half):
                 send.wait_send()
-    for send in [fe_copy] + swaps:
+    for send in [fe_copy] + beside + swaps:
         send.wait_send()
     for store in stores:
         store.wait()
@@ -458,7 +443,7 @@
             pltpu.VMEM((2, BX * 6 * FREQ, LANES), f32),
             pltpu.VMEM((BX * BY, CZ), f32),
             pltpu.VMEM((PAIRS, ROWS, LANES), f32),
-            pltpu.VMEM((2, PAIRS, 8 * WIDE, LANES), f32),
+            pltpu.VMEM((2, PAIRS, 16, LANES), f32),
             pltpu.VMEM((PAIRS, ROWS, LANES), f32),
             pltpu.VMEM((PAIRS - 2, ROWS, LANES), f32),
             pltpu.VMEM((PAIRS, 64, LANES), f32),
@@ -467,18 +452,16 @@
             pltpu.VMEM((COMPS, YY, SUB, LANES), f32),
             pltpu.VMEM((3, YY, SUB, LANES), f32),
             pltpu.VMEM((2, 3, BX, 2 * LANES), f32),
-            pltpu.VMEM((2, 3, SUB, 4 * LANES), f32),
+            pltpu.VMEM((2, 3, BX, 4 * LANES), f32),
             pltpu.VMEM((HY, 3 * BX, LANES), f32),
             pltpu.VMEM((HY, 3 * BX, LANES), f32),
-            pltpu.VMEM((2, 16, 2 * LANES), f32),
             pltpu.VMEM((2, 3, BX, LANES), f32),
-            pltpu.VMEM((2, 2, BX, LANES), f32),
-            pltpu.VMEM((2, 16, 2 * LANES), f32),
             pltpu.VMEM((2, 3, BX, LANES), f32),
-            pltpu.VMEM((2, 2, BX, LANES), f32),
+            pltpu.VMEM((BX, 2 * LANES), f32),
+            pltpu.VMEM((2, BX, 2 * LANES), f32),
             pltpu.SemaphoreType.DMA((13,)),
-            pltpu.SemaphoreType.DMA((20,)),
-            pltpu.SemaphoreType.DMA((20,)),
+            pltpu.SemaphoreType.DMA((16,)),
+            pltpu.SemaphoreType.DMA((16,)),
         ],
         compiler_params=pltpu.CompilerParams(
             collective_id=0, has_side_effects=True, vmem_limit_bytes=24 * 1024 * 1024

time: 40.7 us -> 40.9 us (level)
  no operation moved by 1% of the time
where the time goes in v4:
time: 40.9 us; the launch traced here: 40.7 us
  Pallas kernels  40.1 us (98%)
  between operations  0.64 us (2%)
    pallas_call x1, Pallas kernels, body_fn(): pl.pallas_call(kernel, out_shape=(jax.ShapeDtypeStruct((BX * 6 * FREQ, 2...  39.3 us

profile of v4, /device:TPU:1, one launch (start us, length us, event | category | flops | bytes accessed | tf_op | source)
XLA Modules:
  0.0 40.7 jit_solution(10729888633337934578)
XLA Ops:
  0.6 39.3 %shard_map.121 = (f32[192,256]{1,0:T(8,128)S(1)}, f32[8,256]{1,0:T(8,128)S(1)}, f32[384,48]{1,0:T(8,128)S(1)}) custom-call(f32[384,48]{1,0:T(8,128)} %bitcast.8, f32[384,48]{1,0:T(8,128)} %bitcast.9, s32[128,48]{1,0:T(8,128)} %bitcast.11, f32[4]{0:T(128)} %perm_in.1, s32[3,64]{1,0:T(4,128)} %bitcast.12, f32[3,64]{1,0:T(4,128)} %bitcast.13, f32[4]{0:T(128)} %omegas_in.1, ...), custom_call_target="tpu_custom_call" | custom-call | tf_op jit(solution)/shard_map/pallas_call | solution.py:423
  40.0 0.8 %shard_map.122 = (f32[192,256]{1,0:T(8,128)}, f32[8,256]{1,0:T(8,128)}, f32[384,48]{1,0:T(8,128)}) custom-call(f32[192,256]{1,0:T(8,128)S(1)} %get-tuple-element.9.adj, f32[8,256]{1,0:T(8,128)S(1)} %get-tuple-element.10.grad, f32[384,48]{1,0:T(8,128)S(1)} %get-tuple-element.11.fe), custom_call_target="tpu_custom_call" | custom-call | tf_op jit(solution)/shard_map/pallas_call | solution.py:486

commit v5 on v4

--- a/solution.py
+++ b/solution.py
@@ -164,6 +164,10 @@
             to_low, to_high = pl.ds(1, 5), pl.ds(0, 5)
         sides = ((0, down_x), (1, up_x))
         sends = []
+        sends += [
+            remote(packed.at[last], body.at[at_low], (1, 1 + half), (gx, up_y, 0)),
+            remote(packed.at[first], body.at[at_high], (2, 1 + half), (gx, down_y, 1)),
+        ]
         for side, to_x in sides:
             place = pl.ds(48 * side, 16)
             role = 7 + 2 * side + half
@@ -171,10 +175,6 @@
                 remote(edge.at[side, last], halo.at[at_low, place], (3 + 4 * side, role), (to_x, up_y, 0)),
                 remote(edge.at[side, first], halo.at[at_high, place], (4 + 4 * side, role), (to_x, down_y, 1)),
             ]
-        sends += [
-            remote(packed.at[last], body.at[at_low], (1, 1 + half), (gx, up_y, 0)),
-            remote(packed.at[first], body.at[at_high], (2, 1 + half), (gx, down_y, 1)),
-        ]
         for side, to_x in sides:
             place = pl.ds(48 * side, 16)
             role = 3 + 2 * side + half
@@ -191,6 +191,8 @@
     beside = [remote(sy.at[0], g_y.at[0], (12, 12), below), remote(sy.at[1], g_y.at[1], (13, 13), above)]
 
     pl.semaphore_wait(barrier, len(senders))
+    for send in beside:
+        send.start()
     for half in (0, 1):
         @pl.when(core == half)
         def _(half=half):
@@ -200,8 +202,6 @@
                 body0[2:8] = packed[0:6]
             else:
                 body1[0:5] = packed[3:8]
-    for send in beside:
-        send.start()
 
     y_first = gy * BY + core * HY - WIDE
     row = iota((YY * SUB, 64), 0)

time: 40.9 us -> 41 us (level)
  no operation moved by 1% of the time
where the time goes in v5:
time: 41 us; the launch traced here: 40.8 us
  Pallas kernels  40.2 us (98%)
  between operations  0.64 us (2%)
    pallas_call x1, Pallas kernels, body_fn(): pl.pallas_call(kernel, out_shape=(jax.ShapeDtypeStruct((BX * 6 * FREQ, 2...  39.4 us

profile of v5, /device:TPU:1, one launch (start us, length us, event | category | flops | bytes accessed | tf_op | source)
XLA Modules:
  0.0 40.8 jit_solution(16852304183124289083)
XLA Ops:
  0.6 39.4 %shard_map.121 = (f32[192,256]{1,0:T(8,128)S(1)}, f32[8,256]{1,0:T(8,128)S(1)}, f32[384,48]{1,0:T(8,128)S(1)}) custom-call(f32[384,48]{1,0:T(8,128)} %bitcast.8, f32[384,48]{1,0:T(8,128)} %bitcast.9, s32[128,48]{1,0:T(8,128)} %bitcast.11, f32[4]{0:T(128)} %perm_in.1, s32[3,64]{1,0:T(4,128)} %bitcast.12, f32[3,64]{1,0:T(4,128)} %bitcast.13, f32[4]{0:T(128)} %omegas_in.1, ...), custom_call_target="tpu_custom_call" | custom-call | tf_op jit(solution)/shard_map/pallas_call | solution.py:423
  40.1 0.8 %shard_map.122 = (f32[192,256]{1,0:T(8,128)}, f32[8,256]{1,0:T(8,128)}, f32[384,48]{1,0:T(8,128)}) custom-call(f32[192,256]{1,0:T(8,128)S(1)} %get-tuple-element.9.adj, f32[8,256]{1,0:T(8,128)S(1)} %get-tuple-element.10.grad, f32[384,48]{1,0:T(8,128)S(1)} %get-tuple-element.11.fe), custom_call_target="tpu_custom_call" | custom-call | tf_op jit(solution)/shard_map/pallas_call | solution.py:486

commit v6 on v2

--- a/solution.py
+++ b/solution.py
@@ -49,7 +49,7 @@
     perm, omegas, anchor,
     e_v, h_v, mat_v, cells_v, amps_v, mask_v, fwd_v, adj_v, coef_v,
     packed, edge, body, halo, merged, fields, source, gain, flat,
-    fe_send, fe_recv, g_send, g_x, g_y, g_c,
+    fe_send, g_send, g_x, g_y, g_c,
     load_sem, send_sem, recv_sem,
 ):
     nx, ny = lax.axis_size("gx"), lax.axis_size("gy")
@@ -60,10 +60,8 @@
 
     barrier = pltpu.get_barrier_semaphore()
     face_y = jnp.where(core == 0, down_y, up_y)
-    senders = [(gx, gy, other)]
-    for h in (0, 1):
-        senders += [(up_x, gy, h), (down_x, gy, h)]
-        senders += [(gx, face_y, h), (up_x, face_y, h), (down_x, face_y, h)]
+    senders = [(x, face_y, h) for x in (up_x, down_x, gx) for h in (0, 1)]
+    senders += [(x, gy, h) for x in (up_x, down_x) for h in (0, 1)] + [(gx, gy, other)]
     for sender in senders:
         pl.semaphore_signal(barrier, inc=1, device_id=sender, device_id_type=pl.DeviceIdType.MESH)
 
@@ -129,16 +127,17 @@
         return pl.ds(1 - dest, SENT)
 
     pl.semaphore_wait(barrier, len(senders))
-    sends = [
-        remote(packed.at[PAIRS - 1], body.at[core, 0], (1, 1 + core), (gx, up_y, 0)),
-        remote(packed.at[0], body.at[core, 5], (2, 1 + core), (gx, down_y, 1)),
-    ]
+    sends = []
     for side, to_x in ((0, down_x), (1, up_x)):
         place = pl.ds(48 * side, 16)
         sends += [
             remote(edge.at[side, PAIRS - 1], halo.at[core, 0, place], (3 + 4 * side, 7 + 2 * side + core), (to_x, up_y, 0)),
             remote(edge.at[side, 0], halo.at[core, 5, place], (4 + 4 * side, 7 + 2 * side + core), (to_x, down_y, 1)),
         ]
+    sends += [
+        remote(packed.at[PAIRS - 1], body.at[core, 0], (1, 1 + core), (gx, up_y, 0)),
+        remote(packed.at[0], body.at[core, 5], (2, 1 + core), (gx, down_y, 1)),
+    ]
     for side, to_x in ((0, down_x), (1, up_x)):
         place = pl.ds(48 * side, 16)
         for dest in (0, 1):
@@ -293,25 +292,28 @@
     below = (gx, jnp.where(core == 0, down_y, gy), other)
     first_rows, last_rows = g_send.at[:, pl.ds(0, LANES)], g_send.at[:, pl.ds(LANES, LANES)]
     swaps = [
-        remote(first_rows, g_y.at[0], (12, 12), below),
-        remote(last_rows, g_y.at[1], (13, 13), above),
         remote(first_rows, g_c.at[0, 0], (14, 14), (down_x,) + below[1:]),
         remote(last_rows, g_c.at[0, 1], (15, 15), (down_x,) + above[1:]),
         remote(first_rows, g_c.at[1, 0], (16, 16), (up_x,) + below[1:]),
         remote(last_rows, g_c.at[1, 1], (17, 17), (up_x,) + above[1:]),
+        remote(first_rows, g_y.at[0], (12, 12), below),
+        remote(last_rows, g_y.at[1], (13, 13), above),
         remote(g_send, g_x.at[0], (18, 18), (down_x, gy, core)),
         remote(g_send, g_x.at[1], (19, 19), (up_x, gy, core)),
     ]
     for swap in swaps:
         swap.start()
 
+    fe_rows = fe.reshape(3 * BX * BY, CZ)
     for y in range(HY):
         v = jnp.concatenate([fields[c, 2 + y, 0:BX, :] for c in range(3)], axis=0)
         moved = roll(v, -CZ, 1)
         first = core == 0
-        fe[pl.ds(HY * core + y, 3 * BX, stride=BY), :] = jnp.where(first, v, moved)[:, :CZ]
-        fe_send[y] = jnp.where(first, moved, v)
-    fe_copy = remote(fe_send, fe_recv, (11, 11), (gx, gy, other))
+        fe_rows[pl.ds(HY * core + y, 3 * BX, stride=BY), :] = jnp.where(first, v, moved)[:, :CZ]
+        fe_send[pl.ds(y, 3 * BX, stride=HY), :] = jnp.where(first, moved, v)[:, :CZ]
+    fe_copy = remote(
+        fe_send.reshape(3 * BX, HY, CZ), fe.at[:, pl.ds(HY * core, HY), :], (11, 11), (gx, gy, other)
+    )
     fe_copy.start()
 
     for t in (0, 1):
@@ -329,10 +331,6 @@
     ]
     for store in stores:
         store.start()
-
-    fe_copy.wait_recv()
-    for y in range(HY):
-        fe[pl.ds(HY * other + y, 3 * BX, stride=BY), :] = fe_recv[y][:, :CZ]
 
     for swap in swaps:
         swap.wait_recv()
@@ -359,6 +357,7 @@
         ok = same_pixel(y_row, anchor[1], by)
         result = result + jnp.where(ok, roll(along_x, -SLAB * by, 1)[:, : 2 * LANES], 0.0)
     grad[...] = result
+    remote(fe_send.reshape(3 * BX, HY, CZ), fe.at[:, pl.ds(HY * other, HY), :], (11, 11), (gx, gy, other)).wait_recv()
 
     for send in sends + [fe_copy] + swaps:
         send.wait_send()
@@ -388,7 +387,7 @@
         out_shape=(
             jax.ShapeDtypeStruct((BX * 6 * FREQ, 2 * LANES), f32),
             jax.ShapeDtypeStruct((BX, 2 * LANES), f32),
-            jax.ShapeDtypeStruct((3 * BX * BY, CZ), f32),
+            jax.ShapeDtypeStruct((3 * BX, BY, CZ), f32),
         ),
         in_specs=[anywhere] * 10,
         out_specs=(anywhere, vmem, vmem),
@@ -414,8 +413,7 @@
             pltpu.VMEM((3, YY, SUB, LANES), f32),
             pltpu.VMEM((2, 3, BX, 2 * LANES), f32),
             pltpu.VMEM((2, 3, BX, 2 * LANES), f32),
-            pltpu.VMEM((HY, 3 * BX, LANES), f32),
-            pltpu.VMEM((HY, 3 * BX, LANES), f32),
+            pltpu.VMEM((3 * BX * HY, CZ), f32),
             pltpu.VMEM((BX, 2 * LANES), f32),
             pltpu.VMEM((2, BX, 2 * LANES), f32),
             pltpu.VMEM((2, BX, LANES), f32),

time: 39 us -> 38.9 us (level)
  no operation moved by 1% of the time
where the time goes in v6:
time: 38.9 us; the launch traced here: 38.3 us
  Pallas kernels  37.6 us (97%)
  between operations  0.64 us (2%)
    pallas_call x1, Pallas kernels, body_fn(): pl.pallas_call(kernel, out_shape=(jax.ShapeDtypeStruct((BX * 6 * FREQ, 2...  36.9 us

profile of v6, /device:TPU:1, one launch (start us, length us, event | category | flops | bytes accessed | tf_op | source)
XLA Modules:
  0.0 38.3 jit_solution(8447998750901085786)
XLA Ops:
  0.6 36.9 %shard_map.121 = (f32[192,256]{1,0:T(8,128)S(1)}, f32[8,256]{1,0:T(8,128)S(1)}, f32[24,16,48]{2,1,0:T(8,128)S(1)}) custom-call(f32[384,48]{1,0:T(8,128)} %bitcast.8, f32[384,48]{1,0:T(8,128)} %bitcast.9, s32[128,48]{1,0:T(8,128)} %bitcast.11, f32[4]{0:T(128)} %perm_in.1, s32[3,64]{1,0:T(4,128)} %bitcast.12, f32[3,64]{1,0:T(4,128)} %bitcast.13, f32[4]{0:T(128)} %omegas_in.1, ...), custom_call_target="tpu_custom_call" | custom-call | tf_op jit(solution)/shard_map/pallas_call | solution.py:385
  37.5 0.8 %shard_map.122 = (f32[192,256]{1,0:T(8,128)}, f32[8,256]{1,0:T(8,128)}, f32[24,16,48]{2,1,0:T(8,128)}) custom-call(f32[192,256]{1,0:T(8,128)S(1)} %get-tuple-element.9.adj, f32[8,256]{1,0:T(8,128)S(1)} %get-tuple-element.10.grad, f32[24,16,48]{2,1,0:T(8,128)S(1)} %get-tuple-element.11.fe), custom_call_target="tpu_custom_call" | custom-call | tf_op jit(solution)/shard_map/pallas_call | solution.py:445

commit v7 on v2

--- a/solution.py
+++ b/solution.py
@@ -193,11 +193,9 @@
 
     remote(part(core), body.at[other, span(core)], (0, 0), (gx, gy, other)).wait_recv()
     for h in (0, 1):
-        remote(packed.at[0], body.at[h, 5 * core], (0, 1 + h), (gx, gy, other)).wait_recv()
         for side in (0, 1):
             place = pl.ds(48 * side, 16)
             remote(edge.at[0, pl.ds(0, SENT)], halo.at[h, span(core), place], (0, 3 + 2 * side + h), (gx, gy, other)).wait_recv()
-            remote(edge.at[0, 0], halo.at[h, 5 * core, place], (0, 7 + 2 * side + h), (gx, gy, other)).wait_recv()
 
     x_of = iota((SUB, LANES), 0)
     x_of = gx * BX + jnp.where(x_of < 12, x_of, x_of - SUB)
@@ -213,7 +211,7 @@
         odd = jnp.where(lanes < CZ, roll(low, -CZ, 1), high)
         return even, odd
 
-    for pair in range(YY // 2):
+    def unpack(pair):
         own = merge(body[0, pair], body[1, pair], lane_b)
         beside = merge(halo[0, pair], halo[1, pair], lane_h)
         for k in (0, 1):
@@ -269,8 +267,21 @@
                     out = jnp.where(quarter == q, roll(v, SLAB * q - BOTTOM, 1), out)
                 flat[time, c, :, pl.ds(LANES * tile, LANES)] = out
 
-    magnetic_rows(0, 11)
-    electric_rows(1, 11, 0)
+    for pair in (1, 2, 3, 4):
+        unpack(pair)
+    magnetic_rows(2, 9)
+    electric_rows(3, 9, 0)
+    for h in (0, 1):
+        remote(packed.at[0], body.at[h, 5 * core], (0, 1 + h), (gx, gy, other)).wait_recv()
+        for side in (0, 1):
+            place = pl.ds(48 * side, 16)
+            remote(edge.at[0, 0], halo.at[h, 5 * core, place], (0, 7 + 2 * side + h), (gx, gy, other)).wait_recv()
+    for pair in (0, 5):
+        unpack(pair)
+    magnetic_rows(0, 2)
+    magnetic_rows(9, 11)
+    electric_rows(1, 3, 0)
+    electric_rows(9, 11, 0)
     flatten(0)
     magnetic_rows(1, 10)
     electric_rows(2, 10, 1)

time: 39 us -> 38.8 us (level)
  no operation moved by 1% of the time
where the time goes in v7:
time: 38.8 us; the launch traced here: 38.5 us
  Pallas kernels  37.9 us (98%)
  between operations  0.64 us (2%)
    pallas_call x1, Pallas kernels, body_fn(): pl.pallas_call(kernel, out_shape=(jax.ShapeDtypeStruct((BX * 6 * FREQ, 2...  37.1 us

profile of v7, /device:TPU:1, one launch (start us, length us, event | category | flops | bytes accessed | tf_op | source)
XLA Modules:
  0.0 38.5 jit_solution(10860957410853956897)
XLA Ops:
  0.6 37.1 %shard_map.121 = (f32[192,256]{1,0:T(8,128)S(1)}, f32[8,256]{1,0:T(8,128)S(1)}, f32[384,48]{1,0:T(8,128)S(1)}) custom-call(f32[384,48]{1,0:T(8,128)} %bitcast.8, f32[384,48]{1,0:T(8,128)} %bitcast.9, s32[128,48]{1,0:T(8,128)} %bitcast.11, f32[4]{0:T(128)} %perm_in.1, s32[3,64]{1,0:T(4,128)} %bitcast.12, f32[3,64]{1,0:T(4,128)} %bitcast.13, f32[4]{0:T(128)} %omegas_in.1, ...), custom_call_target="tpu_custom_call" | custom-call | tf_op jit(solution)/shard_map/pallas_call | solution.py:397
  37.8 0.8 %shard_map.122 = (f32[192,256]{1,0:T(8,128)}, f32[8,256]{1,0:T(8,128)}, f32[384,48]{1,0:T(8,128)}) custom-call(f32[192,256]{1,0:T(8,128)S(1)} %get-tuple-element.9.adj, f32[8,256]{1,0:T(8,128)S(1)} %get-tuple-element.10.grad, f32[384,48]{1,0:T(8,128)S(1)} %get-tuple-element.11.fe), custom_call_target="tpu_custom_call" | custom-call | tf_op jit(solution)/shard_map/pallas_call | solution.py:458

commit v8 on v2

--- a/solution.py
+++ b/solution.py
@@ -80,6 +80,8 @@
 
     edge[...] = jnp.zeros_like(edge)
     halo[:, :, 16:48, :] = jnp.zeros((2, YY // 2, 32, LANES), jnp.float32)
+
+    halo[:, 5 * core, pl.ds(48 - 40 * core, 8), :] = jnp.zeros((2, 8, LANES), jnp.float32)
 
     for load in loads[:4]:
         load.wait()
@@ -135,9 +137,12 @@
     ]
     for side, to_x in ((0, down_x), (1, up_x)):
         place = pl.ds(48 * side, 16)
+        whole, near, near_place = pl.ds(0, 16), pl.ds(8 * side, 8), pl.ds(56 * side, 8)
+        to_up, up_place = (near, near_place) if side == 1 else (whole, place)
+        to_down, down_place = (near, near_place) if side == 0 else (whole, place)
         sends += [
-            remote(edge.at[side, PAIRS - 1], halo.at[core, 0, place], (3 + 4 * side, 7 + 2 * side + core), (to_x, up_y, 0)),
-            remote(edge.at[side, 0], halo.at[core, 5, place], (4 + 4 * side, 7 + 2 * side + core), (to_x, down_y, 1)),
+            remote(edge.at[side, PAIRS - 1, to_up], halo.at[core, 0, up_place], (3 + 4 * side, 7 + 2 * side + core), (to_x, up_y, 0)),
+            remote(edge.at[side, 0, to_down], halo.at[core, 5, down_place], (4 + 4 * side, 7 + 2 * side + core), (to_x, down_y, 1)),
         ]
     for side, to_x in ((0, down_x), (1, up_x)):
         place = pl.ds(48 * side, 16)
@@ -197,7 +202,12 @@
         for side in (0, 1):
             place = pl.ds(48 * side, 16)
             remote(edge.at[0, pl.ds(0, SENT)], halo.at[h, span(core), place], (0, 3 + 2 * side + h), (gx, gy, other)).wait_recv()
-            remote(edge.at[0, 0], halo.at[h, 5 * core, place], (0, 7 + 2 * side + h), (gx, gy, other)).wait_recv()
+            for c, rows, at in ((side, 16, 48 * side), (1 - side, 8, 56 * side)):
+                @pl.when(core == c)
+                def _(h=h, side=side, c=c, rows=rows, at=at):
+                    remote(
+                        edge.at[0, 0, pl.ds(0, rows)], halo.at[h, 5 * c, pl.ds(at, rows)], (0, 7 + 2 * side + h), (gx, gy, other)
+                    ).wait_recv()
 
     x_of = iota((SUB, LANES), 0)
     x_of = gx * BX + jnp.where(x_of < 12, x_of, x_of - SUB)

time: 39 us -> 38.5 us (0.987)
  Pallas kernels: 37.7 us -> 37.3 us
    pallas_call x1, Pallas kernels: 37 us -> 36.5 us  [body_fn(): pl.pallas_call(kernel, out_shape=(jax.ShapeDtypeStruct((BX * 6 * FREQ, 2...]
where the time goes in v8:
time: 38.5 us; the launch traced here: 37.9 us
  Pallas kernels  37.3 us (97%)
  between operations  0.64 us (2%)
    pallas_call x1, Pallas kernels, body_fn(): pl.pallas_call(kernel, out_shape=(jax.ShapeDtypeStruct((BX * 6 * FREQ, 2...  36.5 us
    pallas_call x1, Pallas kernels, body_fn(): pl.pallas_call(deliver, out_shape=tuple((jax.ShapeDtypeStruct(v.shape, f3...  0.77 us

profile of v8, /device:TPU:1, one launch (start us, length us, event | category | flops | bytes accessed | tf_op | source)
XLA Modules:
  0.0 37.9 jit_solution(15271636419873204233)
XLA Ops:
  0.6 36.5 %shard_map.121 = (f32[192,256]{1,0:T(8,128)S(1)}, f32[8,256]{1,0:T(8,128)S(1)}, f32[384,48]{1,0:T(8,128)S(1)}) custom-call(f32[384,48]{1,0:T(8,128)} %bitcast.8, f32[384,48]{1,0:T(8,128)} %bitcast.9, s32[128,48]{1,0:T(8,128)} %bitcast.11, f32[4]{0:T(128)} %perm_in.1, s32[3,64]{1,0:T(4,128)} %bitcast.12, f32[3,64]{1,0:T(4,128)} %bitcast.13, f32[4]{0:T(128)} %omegas_in.1, ...), custom_call_target="tpu_custom_call" | custom-call | tf_op jit(solution)/shard_map/pallas_call | solution.py:396
  37.2 0.8 %shard_map.122 = (f32[192,256]{1,0:T(8,128)}, f32[8,256]{1,0:T(8,128)}, f32[384,48]{1,0:T(8,128)}) custom-call(f32[192,256]{1,0:T(8,128)S(1)} %get-tuple-element.9.adj, f32[8,256]{1,0:T(8,128)S(1)} %get-tuple-element.10.grad, f32[384,48]{1,0:T(8,128)S(1)} %get-tuple-element.11.fe), custom_call_target="tpu_custom_call" | custom-call | tf_op jit(solution)/shard_map/pallas_call | solution.py:457
